TPU v7x, 512 devices: a whole 4x8x8 slice. The times are simulated.
512 devices in a mesh: pix: 32 (over z_hi, x, core), mz: 16 (over y, z_lo).
Axes of the slice: x: 4, y: 8, z: 8 (z_hi: 4, z_lo: 2; z = z_hi * 2 + z_lo), core: 2. Of those that a mesh axis runs over, the one named last changes fastest.
Arguments:
- spectra: bfloat16 [128, 256, 2048], P('pix', None, 'mz'), may hold values from -6 to 6
- scores: float32 [128, 16384], P('pix'), may hold values from -6 to 6
- loadings: float32 [2048, 64], P('mz'), may hold values from -0.75 to 0.75
- smooth: float32 [64], replicated, may hold values from 0.3 to 3
- thresholds: float32 [2048], P('mz'), may hold values from 0.1 to 1.5
- across: int32 [128, 256], P('pix'), may hold values from 0 to 3
- down: int32 [128, 256], P('pix'), may hold values from 0 to 3
Outputs:
- score_maps: float32 [128, 16384], P('pix')
- final_loadings: float32 [2048, 64], P('mz')
- sparse_part: bfloat16 [128, 256, 2048], P('pix', None, 'mz')
All inputs are finite; a program needn't handle non-finite values.
Results may differ from a plain program's by a relative error of at most 0.001.
Values sent between devices are 32-bit elements; how exact they have to be, the bound alone decides.
A program may use at most 64 MiB of HBM per device.

v0:
```python
import jax
import jax.numpy as jnp
from jax import lax
from jax.sharding import PartitionSpec as P

ITERS = 3


def from_behind(block, axis, distance):
    devices = range(lax.axis_size(axis))
    route = [(i - distance, i) for i in devices if i - distance in devices]
    return lax.ppermute(block, axis, route)


def extended(cells, sides, width):
    for axis, dim in sides:
        count = lax.axis_size(axis)
        ends = count - 1
        head = lax.slice_in_dim(cells, 0, width, axis=dim)
        tail = lax.slice_in_dim(cells, cells.shape[dim] - width, cells.shape[dim], axis=dim)
        cells = jnp.concatenate(
            [
                lax.ppermute(tail, axis, [(i, (i + 1) % count) for i in range(ends)]),
                cells,
                lax.ppermute(head, axis, [((i + 1) % count, i) for i in range(ends)]),
            ],
            axis=dim,
        )
    return cells


def shards(spectra, scores, loadings, smooth, thresholds, across, down):
    hi = lax.Precision.HIGHEST
    rows, cols, bins = spectra.shape
    rank = loadings.shape[1]
    pixels = rows * cols
    pix_id = lax.axis_index("pix")
    total_rows = rows * lax.axis_size("pix")
    data = spectra.reshape(pixels, bins).astype(jnp.float32)
    above_levels = from_behind(down[rows - 1 :], "pix", 1)
    global_row = pix_id * rows + jnp.arange(rows)
    w_down = jnp.where(
        global_row[:, None] < total_rows - 1, (down.astype(jnp.float32) + 1.0) * 0.25, 0.0
    )
    w_above = jnp.where(pix_id > 0, (above_levels[0].astype(jnp.float32) + 1.0) * 0.25, 0.0)
    col_idx = jnp.arange(cols)[None, :]
    w_right = jnp.where(col_idx < cols - 1, (across.astype(jnp.float32) + 1.0) * 0.25, 0.0)
    u = scores.reshape(pixels, rank)
    v = loadings
    approx = jnp.dot(u, v.T, precision=hi, preferred_element_type=jnp.float32)
    sparse = jnp.zeros_like(data)
    dual = jnp.zeros_like(data)
    for step in range(ITERS):
        resid = approx + sparse - data + dual
        padded = extended(u.reshape(rows, cols * rank), (("pix", 0),), 1)
        u3 = u.reshape(rows, cols, rank)
        nxt = padded[2:].reshape(rows, cols, rank)
        before = padded[0].reshape(cols, rank)
        flow_v = w_down[:, :, None] * (u3 - nxt)
        flow_top = w_above[:, None] * (u3[0] - before)
        lap_v = flow_v + jnp.concatenate([flow_top[None], -flow_v[:-1]], axis=0)
        right = jnp.concatenate([u3[:, 1:], jnp.zeros_like(u3[:, :1])], axis=1)
        flow_h = w_right[:, :, None] * (u3 - right)
        lap_h = flow_h - jnp.concatenate([jnp.zeros_like(flow_h[:, :1]), flow_h[:, :-1]], axis=1)
        lap = ((lap_v + lap_h) * smooth[None, None, :]).reshape(pixels, rank)
        vg_part = jnp.dot(resid.T, u, precision=hi, preferred_element_type=jnp.float32)
        vgrad, usq = lax.psum((vg_part, jnp.sum(u * u)), "pix")
        eta_v = 1.0 / (usq / rank + 1.0)
        grad, vsq = lax.psum(
            (jnp.dot(resid, v, precision=hi, preferred_element_type=jnp.float32), jnp.sum(v * v)),
            "mz",
        )
        eta_u = 1.0 / (vsq / rank + 8.0 * smooth + 1.0)
        u = u - eta_u[None, :] * (grad + lap)
        v = v - eta_v * vgrad
        approx = jnp.dot(u, v.T, precision=hi, preferred_element_type=jnp.float32)
        target = data - approx - dual
        sparse = target - jnp.clip(target, -thresholds[None, :], thresholds[None, :])
        dual = dual + approx + sparse - data
    return (u.reshape(rows, cols * rank), v, sparse.reshape(rows, cols, bins).astype(jnp.bfloat16))


def solution(mesh):
    in_specs = (
        P("pix", None, "mz"),
        P("pix", None),
        P("mz", None),
        P(),
        P("mz"),
        P("pix", None),
        P("pix", None),
    )
    out_specs = (P("pix", None), P("mz", None), P("pix", None, "mz"))
    return jax.shard_map(shards, mesh=mesh, in_specs=in_specs, out_specs=out_specs, check_vma=False)
```

profile of v0, /device:TPU:1, one launch (start us, length us, event | category | flops | bytes accessed | tf_op | source)
XLA Modules:
  0.0 833.8 jit_solution(3436112314571243133)
XLA Ops:
  7.9 4.5 collective-permute-start.1
  12.4 1.0 slice.78
  13.5 2.1 collective-permute-start.2
  15.5 1.2 reshape.157
  17.3 1.4 fusion.13
  18.8 1.0 fusion.14
  21.4 0.8 copy-done
  23.5 4.9 collective-permute-start
  28.6 0.8 collective-permute-done
  29.3 0.8 multiply_reduce_fusion.2
  30.4 139.0 %all-reduce.8 = (f32[128,64]{0,1:T(8,128)S(1)}, f32[]{:T(128)}) all-reduce(f32[128,64]{0,1:T(8,128)S(1)} %fusion.14, f32[]{:T(128)} %get-tuple-element.29), channel_id=1, replica_groups=mesh['pix'=32,'mz'=16] {'pix'}, use_global_device_ids=true, to_apply=%region_5.6 | all-reduce | flops 8193 | bytes 65544 | tf_op jit(solution)/shard_map/psum | solution.py:67
  172.0 28.4 %psum.84 = f32[]{:T(128)} all-reduce(f32[]{:T(128)} %get-tuple-element.33), channel_id=1, replica_groups=mesh['pix'=32,'mz'=16] {'mz'}, use_global_device_ids=true, to_apply=%region_1.2 | all-reduce | flops 1 | bytes 8 | tf_op jit(solution)/shard_map/psum | solution.py:69
  201.2 1.7 multiply_reduce_fusion.1
  202.9 1.0 convert_subtract_fusion.4
  204.4 1.4 fusion.11
  206.0 10.8 %collective-permute-start.4 = (f32[1,16384]{1,0:T(1,128)S(1)}, f32[1,16384]{1,0:T(1,128)S(1)}, u32[]{:S(2)}, u32[]{:S(2)}) collective-permute-start(f32[1,16384]{1,0:T(1,128)S(1)} %slice.86), channel_id=1, source_target_pairs={{0,16},{16,32},{32,48},{48,64},{64,80},{80,96},{96,112},{112,128},... | collective-permute-start | bytes 196616 | tf_op jit(solution)/shard_map/ppermute | solution.py:23
  216.9 135.9 %all-reduce.7 = (f32[128,64]{0,1:T(8,128)S(1)}, f32[]{:T(128)}) all-reduce(f32[128,64]{0,1:T(8,128)S(1)} %fusion.9, f32[]{:T(128)} %get-tuple-element.15), channel_id=1, replica_groups=mesh['pix'=32,'mz'=16] {'pix'}, use_global_device_ids=true, to_apply=%region_11.12 | all-reduce | flops 8193 | bytes 65544 | tf_op jit(solution)/shard_map/psum | solution.py:67
  354.1 24.3 %all-reduce.9 = (f32[]{:T(128)}, f32[]{:T(128)}) all-reduce(f32[]{:T(128)} %get-tuple-element.17, f32[]{:T(128)} %get-tuple-element.13), channel_id=1, replica_groups=mesh['pix'=32,'mz'=16] {'mz'}, use_global_device_ids=true, to_apply=%region_7.8 | all-reduce | flops 2 | bytes 16 | tf_op jit(solution)/shard_map/psum | solution.py:69
  380.2 0.8 reduce.11
  381.5 15.4 %collective-permute-start.3 = (f32[1,16384]{1,0:T(1,128)S(1)}, f32[1,16384]{1,0:T(1,128)S(1)}, u32[]{:S(2)}, u32[]{:S(2)}) collective-permute-start(f32[1,16384]{1,0:T(1,128)S(1)} %slice.83), channel_id=1, source_target_pairs={{16,0},{32,16},{48,32},{64,48},{80,64},{96,80},{112,96},{128,112},... | collective-permute-start | bytes 196616 | tf_op jit(solution)/shard_map/ppermute | solution.py:25
  399.0 132.9 %all-reduce.16.cloned.1.call-done = f32[1024,64]{0,1:T(8,128)} async-done(((f32[1024,64]{0,1:T(8,128)}), f32[1024,64]{0,1:T(8,128)}) %all-reduce.16.cloned.1.call-update) | async-done | bytes 262160 | tf_op jit(solution)/shard_map/psum | solution.py:69
  531.9 1.7 multiply_reduce_fusion
  533.8 13.6 %collective-permute-start.6 = (f32[1,16384]{1,0:T(1,128)S(1)}, f32[1,16384]{1,0:T(1,128)S(1)}, u32[]{:S(2)}, u32[]{:S(2)}) collective-permute-start(f32[1,16384]{1,0:T(1,128)S(1)} %slice.94), channel_id=1, source_target_pairs={{0,16},{16,32},{32,48},{48,64},{64,80},{80,96},{96,112},{112,128},... | collective-permute-start | bytes 196616 | tf_op jit(solution)/shard_map/ppermute | solution.py:23
  547.4 1.8 fusion.2
  549.7 1.4 fusion.15
  551.1 132.6 %all-reduce.6 = (f32[128,64]{0,1:T(8,128)S(1)}, f32[]{:T(128)}) all-reduce(f32[128,64]{0,1:T(8,128)S(1)} %fusion.16, f32[]{:T(128)} %get-tuple-element.11), channel_id=1, replica_groups=mesh['pix'=32,'mz'=16] {'pix'}, use_global_device_ids=true, to_apply=%region_17.18 | all-reduce | flops 8193 | bytes 65544 | tf_op jit(solution)/shard_map/psum | solution.py:67
  684.4 0.8 reduce.12
  685.7 8.5 %collective-permute-start.5 = (f32[1,16384]{1,0:T(1,128)S(1)}, f32[1,16384]{1,0:T(1,128)S(1)}, u32[]{:S(2)}, u32[]{:S(2)}) collective-permute-start(f32[1,16384]{1,0:T(1,128)S(1)} %slice.91), channel_id=1, source_target_pairs={{16,0},{32,16},{48,32},{64,48},{80,64},{96,80},{112,96},{128,112},... | collective-permute-start | bytes 196616 | tf_op jit(solution)/shard_map/ppermute | solution.py:25
  696.3 127.0 %all-reduce.18.cloned.1.call-done = f32[1024,64]{0,1:T(8,128)} async-done(((f32[1024,64]{0,1:T(8,128)}), f32[1024,64]{0,1:T(8,128)}) %all-reduce.18.cloned.1.call-update) | async-done | bytes 262160 | tf_op jit(solution)/shard_map/psum | solution.py:69
  823.2 1.0 multiply_subtract_fusion
  824.5 0.9 reshape.168
  825.5 1.7 subtract_convert_fusion
  (94 shorter events, 14.4 us)
Async XLA Ops:
  7.2 194.0 %all-reduce.14.cloned.1.call-start = ((), (), s32[]{:S(2)}) async-start(), calls=%async_computation | async-start | bytes 524288 | tf_op jit(solution)/shard_map/psum | solution.py:69
  7.9 15.3 %collective-permute-start.1 = (s32[1,256]{1,0:T(1,128)S(1)}, s32[1,256]{1,0:T(1,128)S(1)}, u32[]{:S(2)}, u32[]{:S(2)}) collective-permute-start(s32[1,256]{1,0:T(1,128)S(1)} %slice.77), channel_id=1, source_target_pairs={{0,16},{16,32},{32,48},{48,64},{64,80},{80,96},{96,112},{112,128},... | collective-permute-start | bytes 3080 | tf_op jit(solution)/shard_map/ppermute | solution.py:12
  13.4 3.3 copy-start.1
  13.4 3.3 copy-start.2
  13.5 9.8 %collective-permute-start.2 = (f32[1,16384]{1,0:T(1,128)S(1)}, f32[1,16384]{1,0:T(1,128)S(1)}, u32[]{:S(2)}, u32[]{:S(2)}) collective-permute-start(f32[1,16384]{1,0:T(1,128)S(1)} %slice.78), channel_id=1, source_target_pairs={{0,16},{16,32},{32,48},{48,64},{64,80},{80,96},{96,112},{112,128},... | collective-permute-start | bytes 196616 | tf_op jit(solution)/shard_map/ppermute | solution.py:23
  18.8 513.1 %all-reduce.16.cloned.1.call-start = ((), (), s32[]{:S(2)}) async-start(), calls=%async_computation.1 | async-start | bytes 524288 | tf_op jit(solution)/shard_map/psum | solution.py:69
  19.8 0.7 copy-start.5
  20.5 0.7 copy-start.6
  21.2 0.9 copy-start
  22.5 0.7 copy-start.7
  23.5 5.8 collective-permute-start
  170.5 0.7 copy-start.4
  206.0 173.7 %collective-permute-start.4 = (f32[1,16384]{1,0:T(1,128)S(1)}, f32[1,16384]{1,0:T(1,128)S(1)}, u32[]{:S(2)}, u32[]{:S(2)}) collective-permute-start(f32[1,16384]{1,0:T(1,128)S(1)} %slice.86), channel_id=1, source_target_pairs={{0,16},{16,32},{32,48},{48,64},{64,80},{80,96},{96,112},{112,128},... | collective-permute-start | bytes 196616 | tf_op jit(solution)/shard_map/ppermute | solution.py:23
  379.7 443.6 %all-reduce.18.cloned.1.call-start = ((), (), s32[]{:S(2)}) async-start(), calls=%async_computation.2 | async-start | bytes 524288 | tf_op jit(solution)/shard_map/psum | solution.py:69
  381.5 16.3 %collective-permute-start.3 = (f32[1,16384]{1,0:T(1,128)S(1)}, f32[1,16384]{1,0:T(1,128)S(1)}, u32[]{:S(2)}, u32[]{:S(2)}) collective-permute-start(f32[1,16384]{1,0:T(1,128)S(1)} %slice.83), channel_id=1, source_target_pairs={{16,0},{32,16},{48,32},{64,48},{80,64},{96,80},{112,96},{128,112},... | collective-permute-start | bytes 196616 | tf_op jit(solution)/shard_map/ppermute | solution.py:25
  533.8 150.6 %collective-permute-start.6 = (f32[1,16384]{1,0:T(1,128)S(1)}, f32[1,16384]{1,0:T(1,128)S(1)}, u32[]{:S(2)}, u32[]{:S(2)}) collective-permute-start(f32[1,16384]{1,0:T(1,128)S(1)} %slice.94), channel_id=1, source_target_pairs={{0,16},{16,32},{32,48},{48,64},{64,80},{80,96},{96,112},{112,128},... | collective-permute-start | bytes 196616 | tf_op jit(solution)/shard_map/ppermute | solution.py:23
  685.7 9.3 %collective-permute-start.5 = (f32[1,16384]{1,0:T(1,128)S(1)}, f32[1,16384]{1,0:T(1,128)S(1)}, u32[]{:S(2)}, u32[]{:S(2)}) collective-permute-start(f32[1,16384]{1,0:T(1,128)S(1)} %slice.91), channel_id=1, source_target_pairs={{16,0},{32,16},{48,32},{64,48},{80,64},{96,80},{112,96},{128,112},... | collective-permute-start | bytes 196616 | tf_op jit(solution)/shard_map/ppermute | solution.py:25
  694.2 131.2 %copy-start.3 = (f32[128,64]{0,1:T(8,128)}, f32[128,64]{0,1:T(8,128)S(1)}, u32[]{:S(2)}) copy-start(f32[128,64]{0,1:T(8,128)S(1)} %multiply_subtract_fusion.3) | copy-start | bytes 98308
  824.5 1.0 copy-start.8
Sparse Core Ops, SparseCore 0:
  18.9 136.0 all-reduce.13
  379.8 152.0 all-reduce.15
  684.5 138.6 all-reduce.17
where the time goes:
time: 844 us; the launch traced here: 834 us
  blocking collectives  460 us (55%)
  waiting for transfers between devices  261 us (31%)
  starting transfers between devices  59.9 us (7%)
  between operations  18.3 us (2%)
  local copies, waits for them, and re-layouts  12.4 us (1%)
  matrix products  11.3 us (1%)
  other arithmetic  10.6 us (1%)
    psum x3, blocking collectives, shards(): vgrad, usq = lax.psum((vg_part, jnp.sum(u * u)), 'pix')  407 us
    psum x3, waiting for transfers between devices, shards(): lax.psum((jnp.dot(resid, v, precision=hi, preferred_element_type=jnp.floa...  260 us
    psum x2, blocking collectives, shards(): lax.psum((jnp.dot(resid, v, precision=hi, preferred_element_type=jnp.floa...  52.6 us
    ppermute x3, starting transfers between devices, extended(): lax.ppermute(head, axis, [((i + 1) % count, i) for i in range(ends)])  28.8 us
    ppermute x3, starting transfers between devices, extended(): lax.ppermute(tail, axis, [(i, (i + 1) % count) for i in range(ends)])  26.5 us
  transfers between devices with their start and end apart: 10, of which 5 were waited for; matrix products, arithmetic and copies ran while one was open for 2% of the time, Pallas kernels for 0%

commit v1 on v0

v1 whole, which is shorter than its diff:
```python
import functools
import jax
import jax.numpy as jnp
from jax import lax
from jax.experimental import pallas as pl
from jax.experimental.pallas import tpu as pltpu
from jax.sharding import PartitionSpec as P

ITERS = 3
GROUP = 8
MESH = pl.DeviceIdType.MESH
F32 = jnp.float32
BF16 = jnp.bfloat16
NT = (((1,), (1,)), ((), ()))
TN = (((0,), (0,)), ((), ()))


def mm(a, b, dims=(((1,), (0,)), ((), ()))):
    return lax.dot_general(a, b, dims, preferred_element_type=F32)


def split(a):
    high = a.astype(BF16)
    return high, (a - high.astype(F32)).astype(BF16)


def kernel(
    group,
    x_hbm, u_hbm, v_hbm, smooth_hbm, thr_hbm, across_hbm, down_hbm,
    uo_hbm, vo_hbm, so_hbm,
    x_in, u_in, v_in, smooth_in, thr_in, across_in, down_in, down_above,
    xf, x_e, x_o, c_e, c_o, u_hl, d_h, d_l, b_hh, b_hl, ubuf, vbuf,
    g_send, g_recv, h_send, h_recv, z_recv, halo_send, halo_recv,
    wtmp, shift, weights,
    in_sems, out_sems, g_ssem, g_rsem, u_ssem, u_rsem, h_ssem, h_rsem, z_ssem, z_rsem,
    v_ssem, v_rsem, halo_ssem, halo_rsem, down_ssem, down_rsem,
):
    n_pix, n_mz = lax.axis_size("pix"), lax.axis_size("mz")
    pix, mz = lax.axis_index("pix"), lax.axis_index("mz")
    n_z = n_pix // group
    zed, spot = pix // group, pix % group
    rows, cols, bins = x_in.shape
    rank = v_in.shape[1]
    nq = rows * cols // 2
    piece = nq // n_mz
    pairs = piece // rows
    srows = rank // group
    below, above = (pix + 1) % n_pix, (pix + n_pix - 1) % n_pix

    barrier = pltpu.get_barrier_semaphore()

    def greet(device):
        pl.semaphore_signal(barrier, inc=1, device_id=device, device_id_type=MESH)

    def each(count, act):
        lax.fori_loop(1, count, lambda i, _: (act(i), 0)[1], 0)

    def mz_peer(i):
        return (mz + i) % n_mz

    def group_peer(i):
        return (spot + i) % group

    def z_peer(i):
        return (zed + i) % n_z

    each(n_mz, lambda i: greet((pix, mz_peer(i))))
    each(group, lambda i: greet((zed * group + group_peer(i), mz)))
    each(n_z, lambda i: greet((z_peer(i) * group + spot, mz)))
    greet((below, mz))
    greet((above, mz))

    loads = [
        pltpu.make_async_copy(src, dst, in_sems.at[i])
        for i, (src, dst) in enumerate(
            [
                (u_hbm, u_in), (v_hbm, v_in), (x_hbm, x_in), (down_hbm, down_in),
                (across_hbm, across_in), (smooth_hbm, smooth_in), (thr_hbm, thr_in),
            ]
        )
    ]
    for load in loads:
        load.start()

    def remote(src, dst, ssem, rsem, device):
        return pltpu.make_async_remote_copy(
            src_ref=src, dst_ref=dst, send_sem=ssem, recv_sem=rsem,
            device_id=device, device_id_type=MESH,
        )

    def drain(ref, sem):
        pltpu.make_async_copy(ref, ref, sem).wait()

    def my_rows(base=8):
        return pl.ds(pl.multiple_of(base + piece * mz, 8), piece)

    loads[0].wait()
    zeros8 = jnp.zeros((8, 128), F32)
    for k in range(ITERS + 1):
        ubuf[k, 0:8, :] = zeros8
        ubuf[k, 8 + nq : 16 + nq, :] = zeros8
    for t in range(cols // 2):
        ubuf[0, 8 + rows * t : 8 + rows * (t + 1), :] = u_in[:, 128 * t : 128 * (t + 1)]

    pl.semaphore_wait(barrier, n_mz - 1 + group - 1 + n_z - 1 + 2)

    def halos(k):
        up = remote(
            halo_send.at[k, 0], halo_recv.at[k, 1], halo_ssem.at[k, 0], halo_rsem.at[k, 1],
            (above, mz),
        )
        down = remote(
            halo_send.at[k, 1], halo_recv.at[k, 0], halo_ssem.at[k, 1], halo_rsem.at[k, 0],
            (below, mz),
        )
        return up, down

    def send_halos(k, mine):
        shift[0] = mine
        halo_send[k, 0] = shift[0, pl.ds(0, pairs, stride=rows), :]
        halo_send[k, 1] = shift[0, pl.ds(rows - 1, pairs, stride=rows), :]
        for copy in halos(k):
            copy.start()

    send_halos(0, ubuf[0, my_rows(), :])
    loads[3].wait()
    down_copy = remote(down_in, down_above, down_ssem, down_rsem, (below, mz))
    down_copy.start()

    loads[1].wait()
    vbuf[0] = v_in[...].T
    loads[2].wait()
    xf[...] = x_in[...].reshape(rows * cols, bins).astype(F32)
    for r in range(rows):
        for par, dst in ((0, x_e), (1, x_o)):
            dst[pl.ds(r, cols // 2, stride=rows), :] = xf[
                pl.ds(r * cols + par, cols // 2, stride=2), :
            ]
    for load in loads[4:]:
        load.wait()
    thr = thr_in[...]

    b_hh[...] = jnp.zeros_like(b_hh)
    b_hl[...] = jnp.zeros_like(b_hl)
    chunk = max(128, piece)

    def factors(k):
        high, low = split(vbuf[k])
        for at, part in ((0, high), (128, high)):
            b_hh[at : at + rank, 0:bins] = part
            b_hh[at + rank : at + 2 * rank, bins : 2 * bins] = part
        for at, part in ((0, high), (128, low)):
            b_hl[at : at + rank, 0:bins] = part
            b_hl[at + rank : at + 2 * rank, bins : 2 * bins] = part

    def send_g(k, j):
        return remote(
            g_send.at[k, j], g_recv.at[k, mz], g_ssem.at[k], g_rsem.at[k], (pix, j)
        )

    def sweep(k):
        factors(k)
        usq = jnp.zeros((8, 128), F32)
        vsq = jnp.sum(vbuf[k] * vbuf[k], axis=0, keepdims=True)
        for q in range(0, nq, chunk):
            here = pl.ds(q, chunk)
            u = ubuf[k, q + 8 : q + 8 + chunk, :]
            u_h, u_l = split(u)
            u_hl[here, 0:128] = u_h
            u_hl[here, 128:256] = u_l
            usq = usq + jnp.sum((u * u).reshape(chunk // 8, 8, 128), axis=0)
            approx = mm(u_hl[here, :], b_hh[...]) + mm(u_h, b_hl[128:256, :])
            for par, x, c in ((0, x_e, c_e), (1, x_o, c_o)):
                low = approx[:, par * bins : (par + 1) * bins]
                if k == 0:
                    d = low - x[here, :]
                else:
                    t = x[here, :] - low
                    if k > 1:
                        old = c[here, :]
                        t = t + old
                    clipped = jnp.clip(t, -thr, thr)
                    if k == ITERS:
                        c[here, :] = t - clipped
                        continue
                    c[here, :] = clipped
                    d = -2.0 * clipped
                    if k > 1:
                        d = d + old
                high, low = split(d)
                d_h[here, par * bins : (par + 1) * bins] = high
                d_l[here, par * bins : (par + 1) * bins] = low
            if k == ITERS:
                continue
            g2 = mm(d_h[here, :], b_hl[...], NT)
            g = g2[:, 0:128] + g2[:, 128:256] + mm(d_l[here, :], b_hh[0:128, :], NT)
            for j in range(q // piece, (q + chunk) // piece):
                g_send[k, j, 0:piece, :] = g[j * piece - q : (j + 1) * piece - q, :]
                g_send[k, j, piece : piece + 1, :] = vsq
        return usq

    def gradients(k):
        usq = sweep(k)
        each(n_mz, lambda i: send_g(k, mz_peer(i)).start())
        both = mm(u_hl[...], d_h[...], TN)
        prod = both[0:128, :] + both[128:256, :] + mm(u_hl[:, 0:128], d_l[...], TN)
        h = prod[0:rank, 0:bins] + prod[rank : 2 * rank, bins : 2 * bins]
        for j in range(group):
            h_send[k, j, 0:srows, :] = h[j * srows : (j + 1) * srows, :]
            h_send[k, j, srows : srows + 8, :] = usq
        each(group, lambda i: send_h(k, group_peer(i)).start())

    def send_h(k, j):
        return remote(
            h_send.at[k, j], h_recv.at[k, spot], h_ssem.at[k], h_rsem.at[k],
            (zed * group + j, mz),
        )

    def send_z(k, j):
        return remote(
            z_recv.at[k, zed], z_recv.at[k, zed], z_ssem.at[k], z_rsem.at[k],
            (j * group + spot, mz),
        )

    def v_rows():
        return pl.ds(pl.multiple_of(srows * spot, 8), srows)

    def send_v(k, j):
        return remote(
            vbuf.at[k, v_rows()], vbuf.at[k, v_rows()], v_ssem.at[k - 1], v_rsem.at[k - 1],
            (zed * group + j, mz),
        )

    def send_u(k, j):
        return remote(
            ubuf.at[k, my_rows()], ubuf.at[k, my_rows()], u_ssem.at[k - 1], u_rsem.at[k - 1],
            (pix, j),
        )

    gradients(0)

    down_copy.wait()
    q_col = lax.broadcasted_iota(jnp.int32, (piece, cols), 0) // rows + pairs * mz
    q_row = lax.broadcasted_iota(jnp.int32, (piece, cols), 0) % rows
    col = lax.broadcasted_iota(jnp.int32, (piece, cols), 1)
    p_col = lax.broadcasted_iota(jnp.int32, (cols, 128), 0)
    p_half = lax.broadcasted_iota(jnp.int32, (cols, 128), 1) // 64

    def spread(which, keep, offset):
        pick = jnp.where(keep & ((col + offset) // 2 == q_col), wtmp[...], 0.0)
        place = jnp.where((p_col + offset) % 2 == p_half, 0.25, 0.0)
        weights[which] = mm(pick.astype(BF16), place.astype(BF16))

    levels = across_in[...].astype(F32) + 1.0
    for t in range(pairs):
        wtmp[rows * t : rows * (t + 1), :] = levels
    spread(0, col < cols - 1, 0)
    spread(1, col < cols - 1, 1)
    levels = down_in[...].astype(F32) + 1.0
    for t in range(pairs):
        wtmp[rows * t : rows * (t + 1), :] = levels
    spread(2, (q_row < rows - 1) | (pix < n_pix - 1), 0)
    for t in range(pairs):
        wtmp[rows * t : rows * t + 1, :] = down_above[rows - 1 : rows, :].astype(F32) + 1.0
        wtmp[rows * t + 1 : rows * (t + 1), :] = levels[0 : rows - 1, :]
    spread(3, (q_row > 0) | (pix > 0), 0)

    smooth = jnp.concatenate([smooth_in[...], smooth_in[...]], axis=1)
    lane = lax.broadcasted_iota(jnp.int32, (piece, 128), 1)

    def laplace(k):
        for copy in halos(k):
            copy.wait()
        window = ubuf[k, pl.ds(pl.multiple_of(piece * mz, 8), piece + 16), :]
        mine = window[8 : 8 + piece]
        swapped = pltpu.roll(mine, 64, 1)
        before = pltpu.roll(window[8 - rows : 8 - rows + piece], 64, 1)
        after = pltpu.roll(window[8 + rows : 8 + rows + piece], 64, 1)
        right = jnp.where(lane < 64, swapped, after)
        left = jnp.where(lane < 64, before, swapped)
        shift[0] = window[7 : 7 + piece]
        shift[1] = window[9 : 9 + piece]
        shift[0, pl.ds(0, pairs, stride=rows), :] = halo_recv[k, 0]
        shift[1, pl.ds(rows - 1, pairs, stride=rows), :] = halo_recv[k, 1]
        flow = weights[0] * (mine - right) + weights[1] * (mine - left)
        flow = flow + weights[2] * (mine - shift[1]) + weights[3] * (mine - shift[0])
        return mine, flow * smooth

    for k in range(ITERS):
        mine, lap = laplace(k)
        drain(h_recv.at[k, pl.ds(0, group - 1)], h_rsem.at[k])
        h_recv[k, spot] = h_send[k, spot]
        total = h_recv[k, 0]
        for j in range(1, group):
            total = total + h_recv[k, j]
        z_recv[k, zed] = total
        each(n_z, lambda i: send_z(k, z_peer(i)).start())
        drain(z_recv.at[k, pl.ds(0, n_z - 1)], z_rsem.at[k])
        total = z_recv[k, 0]
        for j in range(1, n_z):
            total = total + z_recv[k, j]
        usq = jnp.sum(total[srows:, :])
        eta_v = 1.0 / (jnp.full((1, 128), usq, F32) / rank + 1.0)
        vbuf[k + 1, v_rows(), :] = vbuf[k, v_rows(), :] - eta_v * total[0:srows, :]
        each(group, lambda i: send_v(k + 1, group_peer(i)).start())
        drain(g_recv.at[k, pl.ds(0, n_mz - 1)], g_rsem.at[k])
        g_recv[k, mz] = g_send[k, mz]
        total = g_recv[k, 0]
        for j in range(1, n_mz):
            total = total + g_recv[k, j]
        vsq = jnp.sum(total[piece:, :])
        eta_u = 1.0 / (jnp.full((1, 128), vsq, F32) / rank + 8.0 * smooth + 1.0)
        mine = mine - eta_u * (total[0:piece, :] + lap)
        ubuf[k + 1, my_rows(), :] = mine
        each(n_mz, lambda i: send_u(k + 1, mz_peer(i)).start())
        if k + 1 < ITERS:
            send_halos(k + 1, mine)
        drain(vbuf.at[k + 1, pl.ds(0, srows * (group - 1))], v_rsem.at[k])
        drain(ubuf.at[k + 1, pl.ds(8, piece * (n_mz - 1))], u_rsem.at[k])
        if k + 1 < ITERS:
            gradients(k + 1)

    for t in range(cols // 2):
        u_in[:, 128 * t : 128 * (t + 1)] = ubuf[ITERS, 8 + rows * t : 8 + rows * (t + 1), :]
    out_u = pltpu.make_async_copy(u_in, uo_hbm, out_sems.at[0])
    out_u.start()
    v_in[...] = vbuf[ITERS].T
    out_v = pltpu.make_async_copy(v_in, vo_hbm, out_sems.at[1])
    out_v.start()
    sweep(ITERS)
    for r in range(rows):
        for par, src in ((0, c_e), (1, c_o)):
            xf[pl.ds(r * cols + par, cols // 2, stride=2), :] = src[
                pl.ds(r, cols // 2, stride=rows), :
            ]
    x_in[...] = xf[...].astype(BF16).reshape(rows, cols, bins)
    out_s = pltpu.make_async_copy(x_in, so_hbm, out_sems.at[2])
    out_s.start()

    for k in range(ITERS):
        drain(g_send.at[k, pl.ds(0, n_mz - 1)], g_ssem.at[k])
        drain(h_send.at[k, pl.ds(0, group - 1)], h_ssem.at[k])
        drain(z_recv.at[k, pl.ds(0, n_z - 1)], z_ssem.at[k])
        drain(vbuf.at[k, pl.ds(0, srows * (group - 1))], v_ssem.at[k])
        drain(ubuf.at[k, pl.ds(8, piece * (n_mz - 1))], u_ssem.at[k])
    out_u.wait()
    out_v.wait()
    out_s.wait()


def shards(group, spectra, scores, loadings, smooth, thresholds, across, down):
    rows, cols, bins = spectra.shape
    rank = loadings.shape[1]
    n_pix, n_mz = lax.axis_size("pix"), lax.axis_size("mz")
    nq = rows * cols // 2
    piece = nq // n_mz
    pairs = piece // rows
    srows = rank // group
    n_z = n_pix // group
    anywhere = pl.BlockSpec(memory_space=pl.ANY)
    dma = pltpu.SemaphoreType.DMA
    vmem = pltpu.VMEM
    args = (
        spectra, scores, loadings, smooth.reshape(1, rank), thresholds.reshape(1, bins),
        across, down,
    )
    return pl.pallas_call(
        functools.partial(kernel, group),
        out_shape=(
            jax.ShapeDtypeStruct(scores.shape, F32),
            jax.ShapeDtypeStruct(loadings.shape, F32),
            jax.ShapeDtypeStruct(spectra.shape, BF16),
        ),
        in_specs=[anywhere] * 7,
        out_specs=(anywhere,) * 3,
        scratch_shapes=[
            vmem(spectra.shape, BF16),
            vmem(scores.shape, F32),
            vmem(loadings.shape, F32),
            vmem((1, rank), F32),
            vmem((1, bins), F32),
            vmem(across.shape, jnp.int32),
            vmem(down.shape, jnp.int32),
            vmem(down.shape, jnp.int32),
            vmem((rows * cols, bins), F32),
            vmem((nq, bins), F32),
            vmem((nq, bins), F32),
            vmem((nq, bins), F32),
            vmem((nq, bins), F32),
            vmem((nq, 256), BF16),
            vmem((nq, 2 * bins), BF16),
            vmem((nq, 2 * bins), BF16),
            vmem((256, 2 * bins), BF16),
            vmem((256, 2 * bins), BF16),
            vmem((ITERS + 1, nq + 16, 128), F32),
            vmem((ITERS + 1, rank, bins), F32),
            vmem((ITERS, n_mz, piece + 1, 128), F32),
            vmem((ITERS, n_mz, piece + 1, 128), F32),
            vmem((ITERS, group, srows + 8, 128), F32),
            vmem((ITERS, group, srows + 8, 128), F32),
            vmem((ITERS, n_z, srows + 8, 128), F32),
            vmem((ITERS, 2, pairs, 128), F32),
            vmem((ITERS, 2, pairs, 128), F32),
            vmem((piece, cols), F32),
            vmem((2, piece, 128), F32),
            vmem((4, piece, 128), F32),
            dma((7,)),
            dma((3,)),
            dma((ITERS,)),
            dma((ITERS,)),
            dma((ITERS,)),
            dma((ITERS,)),
            dma((ITERS,)),
            dma((ITERS,)),
            dma((ITERS,)),
            dma((ITERS,)),
            dma((ITERS,)),
            dma((ITERS,)),
            dma((ITERS, 2)),
            dma((ITERS, 2)),
            dma,
            dma,
        ],
        compiler_params=pltpu.CompilerParams(
            collective_id=0, has_side_effects=True, vmem_limit_bytes=32 * 1024 * 1024
        ),
        cost_estimate=pl.CostEstimate(
            flops=2 * 10 * rows * cols * bins * rank * 3,
            bytes_accessed=2 * (spectra.size * 2 + scores.size * 4),
            transcendentals=0,
        ),
    )(*args)


def solution(mesh, group=GROUP):
    in_specs = (
        P("pix", None, "mz"),
        P("pix", None),
        P("mz", None),
        P(),
        P("mz"),
        P("pix", None),
        P("pix", None),
    )
    out_specs = (P("pix", None), P("mz", None), P("pix", None, "mz"))
    return jax.shard_map(
        functools.partial(shards, group), mesh=mesh, in_specs=in_specs, out_specs=out_specs,
        check_vma=False,
    )
```

time: 844 us -> 79.6 us (0.09); the launches traced: 834 us -> 79.4 us
  blocking collectives: 460 us -> 0 us
  waiting for transfers between devices: 261 us -> 0 us
  Pallas kernels: 0 us -> 73.8 us
  starting transfers between devices: 59.9 us -> 0 us
  between operations: 18.3 us -> 0.72 us
  matrix products: 11.3 us -> 0 us
  other arithmetic: 10.6 us -> 0 us
    psum x5 -> x0, blocking collectives: 460 us -> none  [the longest x3 407 us: shards(): vgrad, usq = lax.psum((vg_part, jnp.sum(u * u)), 'pix')]
    psum x3 -> x0, waiting for transfers between devices: 260 us -> none  [shards(): lax.psum((jnp.dot(resid, v, precision=hi, preferred_element_type=jnp.floa...]
    pallas_call x0 -> x1, Pallas kernels: none -> 73.8 us  [shards(): pl.pallas_call(functools.partial(kernel, group), out_shape=(jax.ShapeDtyp...]
    ppermute x7 -> x0, starting transfers between devices: 59.8 us -> none  [the longest x3 28.8 us: extended(): lax.ppermute(head, axis, [((i + 1) % count, i) for i in range(ends)])]
    dot_general x10 -> x0, matrix products: 11.3 us -> none  [the longest x4 5.13 us: shards(): approx = jnp.dot(u, v.T, precision=hi, preferred_element_type=jnp.float32)]
  transfers between devices with their start and end apart: 10 -> 0, of which waited for: 5 -> 0; matrix products, arithmetic and copies ran while one was open for 2% -> 0% of each run, Pallas kernels for 0% -> 0%
where the time goes in v1:
time: 79.6 us; the launch traced here: 79.4 us
  Pallas kernels  73.8 us (93%)
  local copies, waits for them, and re-layouts  4.89 us (6%)
    pallas_call x1, Pallas kernels, shards(): pl.pallas_call(functools.partial(kernel, group), out_shape=(jax.ShapeDtyp...  73.8 us
    unnamed x15, local copies, waits for them, and re-layouts  4.19 us

profile of v1, /device:TPU:1, one launch (start us, length us, event | category | flops | bytes accessed | tf_op | source)
XLA Modules:
  0.0 79.4 jit_solution(14916888532381242143)
XLA Ops:
  0.6 0.0 copy-start.2
  0.6 0.0 copy-start.3
  0.7 0.0 copy-start.4
  0.7 0.0 copy-start.5
  0.7 0.9 %copy.10.v_hbm = f32[128,64]{1,0:T(8,128)S(1)} copy(f32[128,64]{0,1:T(8,128)} %param.9) | data formatting | bytes 65536 | tf_op args[2]
  1.5 0.0 copy-done.2
  1.6 0.0 copy-done.3
  1.6 0.0 copy-done.4
  1.6 0.0 copy-done.5
  1.6 0.0 copy-start
  1.6 0.9 %copy-done = bf16[4,256,128]{2,1,0:T(8,128)(2,1)S(1)} copy-done((bf16[4,256,128]{2,1,0:T(8,128)(2,1)S(1)}, bf16[4,256,128]{2,1,0:T(8,128)(2,1)}, u32[]{:S(2)}) %copy-start) | copy-done | bytes 262168
  2.5 0.0 copy-start.1
  2.5 0.9 %copy-done.1 = f32[4,16384]{1,0:T(4,128)S(1)} copy-done((f32[4,16384]{1,0:T(4,128)S(1)}, f32[4,16384]{1,0:T(4,128)}, u32[]{:S(2)}) %copy-start.1) | copy-done | bytes 262168
  3.5 73.8 %shard_map.94 = (f32[4,16384]{1,0:T(4,128)S(1)}, f32[128,64]{1,0:T(8,128)S(1)}, bf16[4,256,128]{2,1,0:T(8,128)(2,1)S(1)}) custom-call(bf16[4,256,128]{2,1,0:T(8,128)(2,1)S(1)} %copy-done, f32[4,16384]{1,0:T(4,128)S(1)} %copy-done.1, f32[128,64]{1,0:T(8,128)S(1)} %copy.10.v_hbm, f32[1,64]{1,0:T(1,128)S(1)} %bitcast.2, f32[1,128]{1,0:T(1,128)S(1)} %bitcast.3, ...), custom_call_target="tpu_custom_call" | custom-call | flops 503316480 | bytes 1048576 | tf_op jit(solution)/shard_map/pallas_call | solution.py:367
  77.3 0.7 copy.11
  78.0 0.7 copy.14
  78.7 0.7 copy.15
Async XLA Ops:
  0.6 0.9 %copy-start.2 = (s32[4,256]{1,0:T(4,128)S(1)}, s32[4,256]{1,0:T(4,128)}, u32[]{:S(2)}) copy-start(s32[4,256]{1,0:T(4,128)} %across_hbm.1) | copy-start | bytes 12292
  0.6 0.9 %copy-start.3 = (s32[4,256]{1,0:T(4,128)S(1)}, s32[4,256]{1,0:T(4,128)}, u32[]{:S(2)}) copy-start(s32[4,256]{1,0:T(4,128)} %down_hbm.1) | copy-start | bytes 12292
  0.7 0.9 %copy-start.4 = (f32[64]{0:T(128)S(1)}, f32[64]{0:T(128)}, u32[]{:S(2)}) copy-start(f32[64]{0:T(128)} %param.10) | copy-start | bytes 772
  0.7 0.9 %copy-start.5 = (f32[128]{0:T(128)S(1)}, f32[128]{0:T(128)}, u32[]{:S(2)}) copy-start(f32[128]{0:T(128)} %param.11) | copy-start | bytes 1540
  1.6 1.0 %copy-start = (bf16[4,256,128]{2,1,0:T(8,128)(2,1)S(1)}, bf16[4,256,128]{2,1,0:T(8,128)(2,1)}, u32[]{:S(2)}) copy-start(bf16[4,256,128]{2,1,0:T(8,128)(2,1)} %x_hbm.1) | copy-start | bytes 786436
  2.5 0.9 %copy-start.1 = (f32[4,16384]{1,0:T(4,128)S(1)}, f32[4,16384]{1,0:T(4,128)}, u32[]{:S(2)}) copy-start(f32[4,16384]{1,0:T(4,128)} %u_hbm.1) | copy-start | bytes 786436

commit v2 on v1

v2 whole, which is shorter than its diff:
```python
import functools
import jax
import jax.numpy as jnp
from jax import lax
from jax.experimental import pallas as pl
from jax.experimental.pallas import tpu as pltpu
from jax.sharding import PartitionSpec as P

ITERS = 3
GROUP = 8
MESH = pl.DeviceIdType.MESH
F32 = jnp.float32
BF16 = jnp.bfloat16
NT = (((1,), (1,)), ((), ()))
TN = (((0,), (0,)), ((), ()))


def mm(a, b, dims=(((1,), (0,)), ((), ()))):
    return lax.dot_general(a, b, dims, preferred_element_type=F32)


def split(a):
    high = a.astype(BF16)
    return high, (a - high.astype(F32)).astype(BF16)


def kernel(
    group,
    x_hbm, u_hbm, v_hbm, smooth_hbm, thr_hbm, across_hbm, down_hbm,
    uo_ref, vo_ref, so_ref,
    x_in, u_in, v_in, smooth_in, thr_in, across_in, down_in, down_above,
    xf, x_own, x_other, c_own, c_other, u_hl, d_h, d_l, b_hh, b_hl, ubuf, vbuf, thr_other,
    g_send, g_recv, h_send, h_recv, z_recv, halo_send, halo_recv,
    wtmp, shift, weights,
    in_sems, out_sems, g_ssem, g_rsem, u_ssem, u_rsem, h_ssem, h_rsem, z_ssem, z_rsem,
    v_ssem, v_rsem, halo_ssem, halo_rsem, down_ssem, down_rsem, thr_ssem, thr_rsem,
    x_ssem, x_rsem, c_ssem, c_rsem,
):
    n_pix, n_mz = lax.axis_size("pix"), lax.axis_size("mz")
    pix, mz = lax.axis_index("pix"), lax.axis_index("mz")
    n_z, n_y, n_team = n_pix // group, n_mz // 2, 2 * group
    zed, spot = pix // group, pix % group
    y, side = mz // 2, mz % 2
    strip, seat = side * n_y + y, side * group + spot
    twin = (pix, 2 * y + 1 - side)
    rows, cols, bins = x_in.shape
    rank = v_in.shape[0]
    nq = rows * cols // 2
    half = nq // 2
    piece = nq // n_mz
    pairs = piece // rows
    srows = rank // group
    below, above = (pix + 1) % n_pix, (pix + n_pix - 1) % n_pix

    barrier = pltpu.get_barrier_semaphore()

    def greet(device):
        pl.semaphore_signal(barrier, inc=1, device_id=device, device_id_type=MESH)

    def each(count, act):
        lax.fori_loop(0, count, lambda i, _: (act(i), 0)[1], 0)

    def far_first(at, i, n):
        return (at + n // 2 + ((i + 1) // 2) * (1 - 2 * (i % 2)) + n) % n

    def y_peer(i):
        return far_first(y, i, n_y)

    def mz_peer(i):
        return 2 * y_peer(i // 2) + (side + 1 - i % 2) % 2

    def team_peer(i):
        return (seat + i + 1) % n_team

    def team_device(j):
        return (zed * group + j % group, 2 * y + j // group)

    def group_peer(i):
        return side * group + (spot + i + 1) % group

    def z_peer(i):
        return (zed + i + 1) % n_z

    def strip_device(j):
        return (pix, 2 * (j % n_y) + j // n_y)

    loads = [
        pltpu.make_async_copy(src, dst, in_sems.at[i])
        for i, (src, dst) in enumerate(
            [
                (u_hbm, u_in), (v_hbm, v_in), (x_hbm, x_in), (thr_hbm, thr_in),
                (down_hbm, down_in), (across_hbm, across_in), (smooth_hbm, smooth_in),
            ]
        )
    ]
    for load in loads:
        load.start()

    each(n_mz - 1, lambda i: greet((pix, mz_peer(i))))
    each(n_team - 1, lambda i: greet(team_device(team_peer(i))))
    each(n_z - 1, lambda i: greet((z_peer(i) * group + spot, mz)))
    greet((below, mz))
    greet((above, mz))

    def remote(src, dst, ssem, rsem, device):
        return pltpu.make_async_remote_copy(
            src_ref=src, dst_ref=dst, send_sem=ssem, recv_sem=rsem,
            device_id=device, device_id_type=MESH,
        )

    def drain(ref, sem):
        pltpu.make_async_copy(ref, ref, sem).wait()

    def my_rows():
        return pl.ds(pl.multiple_of(8 + piece * strip, 8), piece)

    def half_rows(which, at=0, count=half):
        return pl.ds(pl.multiple_of(half * which + at, 8), count)

    zeros8 = jnp.zeros((8, 128), F32)
    ubuf[0, 0:8, :] = zeros8
    ubuf[0, 8 + nq : 16 + nq, :] = zeros8
    b_hh[...] = jnp.zeros_like(b_hh)
    b_hl[...] = jnp.zeros_like(b_hl)
    for load in loads[:4]:
        load.wait()
    for t in range(cols // 2):
        ubuf[0, 8 + rows * t : 8 + rows * (t + 1), :] = u_in[:, 128 * t : 128 * (t + 1)]
    vbuf[0, side] = v_in[...]
    xf[...] = x_in[...].reshape(rows * cols, bins).astype(F32)
    for r in range(rows):
        for par in range(2):
            x_own[par, pl.ds(r, cols // 2, stride=rows), :] = xf[
                pl.ds(r * cols + par, cols // 2, stride=2), :
            ]

    def halos(k):
        to = ((above, mz), (below, mz), strip_device((strip + n_mz - 1) % n_mz),
              strip_device((strip + 1) % n_mz))
        return [
            remote(
                halo_send.at[k, i], halo_recv.at[k, i ^ 1], halo_ssem.at[k, i],
                halo_rsem.at[k, i ^ 1], to[i],
            )
            for i in range(2 if k == 0 else 4)
        ]

    def send_halos(k, mine):
        shift[0] = mine
        halo_send[k, 0, 0:pairs, :] = shift[0, pl.ds(0, pairs, stride=rows), :]
        halo_send[k, 1, 0:pairs, :] = shift[0, pl.ds(rows - 1, pairs, stride=rows), :]
        halo_send[k, 2, 0:8, :] = mine[0:8]
        halo_send[k, 3, 0:8, :] = mine[piece - 8 : piece]
        for copy in halos(k):
            copy.start()

    chunk = 128

    def factors(k, slot):
        high, low = split(vbuf[k, side if slot == 0 else 1 - side])
        for at, part in ((0, high), (128, high)):
            b_hh[slot, at : at + rank, 0:bins] = part
            b_hh[slot, at + rank : at + 2 * rank, bins : 2 * bins] = part
        for at, part in ((0, high), (128, low)):
            b_hl[slot, at : at + rank, 0:bins] = part
            b_hl[slot, at + rank : at + 2 * rank, bins : 2 * bins] = part

    def sweep(k):
        paired = 0 < k < ITERS
        slots = (0, 1) if paired else (0,)
        vsq = jnp.zeros((1, 128), F32)
        for slot in slots:
            factors(k, slot)
            v = vbuf[k, side if slot == 0 else 1 - side]
            vsq = vsq + jnp.sum(v * v, axis=0, keepdims=True)
        usq = zeros8
        for q in range(0, half if paired else nq, chunk):
            here = pl.ds(q, chunk)
            own = half_rows(side, q, chunk) if paired else here
            u = ubuf[k, pl.ds(pl.multiple_of(own.start + 8, 8), chunk), :]
            u_h, u_l = split(u)
            u_hl[here, 0:128] = u_h
            u_hl[here, 128:256] = u_l
            usq = usq + jnp.sum((u * u).reshape(chunk // 8, 8, 128), axis=0)
            g = None
            for slot in slots:
                approx = mm(u_hl[here, :], b_hh[slot]) + mm(u_h, b_hl[slot, 128:256, :])
                thr = (thr_other if slot else thr_in)[...]
                x, c = (x_other, c_other) if slot else (x_own, c_own)
                spot_rows = here if slot else own
                dest = pl.ds(slot * half + q, chunk)
                for par in range(2):
                    lanes = slice(par * bins, (par + 1) * bins)
                    low = approx[:, lanes]
                    data = x[par, spot_rows, :]
                    if k == 0:
                        d = low - data
                    else:
                        t = data - low
                        if k > 1:
                            old = c[par, spot_rows, :]
                            t = t + old
                        clipped = jnp.clip(t, -thr, thr)
                        if k == ITERS:
                            c[par, spot_rows, :] = t - clipped
                            continue
                        c[par, spot_rows, :] = clipped
                        d = -2.0 * clipped
                        if k > 1:
                            d = d + old
                    high, low = split(d)
                    d_h[dest, lanes] = high
                    d_l[dest, lanes] = low
                if k == ITERS:
                    continue
                g2 = mm(d_h[dest, :], b_hl[slot], NT)
                part = g2[:, 0:128] + g2[:, 128:256] + mm(d_l[dest, :], b_hh[slot, 0:128, :], NT)
                g = part if g is None else g + part
            if k == ITERS:
                continue
            for j in range(q // piece, (q + chunk) // piece):
                g_send[k, j, 0:piece, :] = g[j * piece - q : (j + 1) * piece - q, :]
                g_send[k, j, piece : piece + 1, :] = vsq
        return usq

    def send_g(k, i):
        if k == 0:
            to = mz_peer(i)
            return remote(
                g_send.at[k, (to % 2) * n_y + to // 2], g_recv.at[k, mz], g_ssem.at[k],
                g_rsem.at[k], (pix, to),
            )
        to = y_peer(i)
        return remote(
            g_send.at[k, to], g_recv.at[k, y], g_ssem.at[k], g_rsem.at[k], (pix, 2 * to + side)
        )

    def send_h(k, j):
        return remote(
            h_send.at[k, j], h_recv.at[k, seat], h_ssem.at[k], h_rsem.at[k], team_device(j)
        )

    def send_z(k, j):
        return remote(
            z_recv.at[k, zed], z_recv.at[k, zed], z_ssem.at[k], z_rsem.at[k],
            (j * group + spot, mz),
        )

    def v_rows():
        return pl.ds(pl.multiple_of(srows * spot, 8), srows)

    def send_v(k, j):
        ref = vbuf.at[k, side, v_rows()]
        return remote(ref, ref, v_ssem.at[k - 1], v_rsem.at[k - 1], team_device(j))

    def send_u(k, to):
        ref = ubuf.at[k, my_rows()]
        return remote(ref, ref, u_ssem.at[k - 1], u_rsem.at[k - 1], (pix, to))

    def g_count(k):
        return n_mz if k == 0 else n_y

    def h_count(k):
        return group if k == 0 else n_team

    def u_count(k):
        return n_mz if k == ITERS else n_y

    def v_count(k):
        return group if k == ITERS else n_team

    def start_g(k):
        each(g_count(k) - 1, lambda i: send_g(k, i).start())

    def h_part(k, usq):
        for slot in (0,) if k == 0 else (0, 1):
            n = nq if k == 0 else half
            dest = slice(slot * half, slot * half + n)
            both = mm(u_hl[0:n, :], d_h[dest, :], TN)
            prod = both[0:128, :] + both[128:256, :] + mm(u_hl[0:n, 0:128], d_l[dest, :], TN)
            h = prod[0:rank, 0:bins] + prod[rank : 2 * rank, bins : 2 * bins]
            whose = side if slot == 0 else 1 - side
            for j in range(group):
                h_send[k, whose * group + j, 0:srows, :] = h[j * srows : (j + 1) * srows, :]
                h_send[k, whose * group + j, srows : srows + 8, :] = usq
        peer = group_peer if k == 0 else team_peer
        each(h_count(k) - 1, lambda i: send_h(k, peer(i)).start())

    usq = sweep(0)

    pl.semaphore_wait(barrier, n_mz - 1 + n_team - 1 + n_z - 1 + 2)
    start_g(0)
    h_part(0, usq)
    send_halos(0, ubuf[0, my_rows(), :])
    thr_copy = remote(thr_in, thr_other, thr_ssem, thr_rsem, twin)
    thr_copy.start()
    loads[4].wait()
    down_copy = remote(down_in, down_above, down_ssem, down_rsem, (below, mz))
    down_copy.start()
    x_copies = [
        remote(
            x_own.at[par, half_rows(1 - side)], x_other.at[par], x_ssem.at[par], x_rsem.at[par],
            twin,
        )
        for par in range(2)
    ]
    for copy in x_copies:
        copy.start()
    c_copies = [
        remote(
            c_other.at[par], c_own.at[par, half_rows(side)], c_ssem.at[par], c_rsem.at[par],
            twin,
        )
        for par in range(2)
    ]

    for load in loads[5:]:
        load.wait()
    q_col = lax.broadcasted_iota(jnp.int32, (piece, cols), 0) // rows + pairs * strip
    q_row = lax.broadcasted_iota(jnp.int32, (piece, cols), 0) % rows
    col = lax.broadcasted_iota(jnp.int32, (piece, cols), 1)
    p_col = lax.broadcasted_iota(jnp.int32, (cols, 128), 0)
    p_half = lax.broadcasted_iota(jnp.int32, (cols, 128), 1) // 64

    def spread(which, keep, offset):
        pick = jnp.where(keep & ((col + offset) // 2 == q_col), wtmp[...], 0.0)
        place = jnp.where((p_col + offset) % 2 == p_half, 0.25, 0.0)
        weights[which] = mm(pick.astype(BF16), place.astype(BF16))

    levels = across_in[...].astype(F32) + 1.0
    for t in range(pairs):
        wtmp[rows * t : rows * (t + 1), :] = levels
    spread(0, col < cols - 1, 0)
    spread(1, col < cols - 1, 1)
    levels = down_in[...].astype(F32) + 1.0
    for t in range(pairs):
        wtmp[rows * t : rows * (t + 1), :] = levels
    spread(2, (q_row < rows - 1) | (pix < n_pix - 1), 0)
    down_copy.wait()
    for t in range(pairs):
        wtmp[rows * t : rows * t + 1, :] = down_above[rows - 1 : rows, :].astype(F32) + 1.0
        wtmp[rows * t + 1 : rows * (t + 1), :] = levels[0 : rows - 1, :]
    spread(3, (q_row > 0) | (pix > 0), 0)

    smooth = jnp.concatenate([smooth_in[...], smooth_in[...]], axis=1)
    lane = lax.broadcasted_iota(jnp.int32, (piece, 128), 1)

    def laplace(k):
        for copy in halos(k):
            copy.wait()
        if k == 0:
            window = ubuf[k, pl.ds(pl.multiple_of(piece * strip, 8), piece + 16), :]
        else:
            window = jnp.concatenate(
                [halo_recv[k, 2, 0:8, :], ubuf[k, my_rows(), :], halo_recv[k, 3, 0:8, :]], axis=0
            )
        mine = window[8 : 8 + piece]
        swapped = pltpu.roll(mine, 64, 1)
        before = pltpu.roll(window[8 - rows : 8 - rows + piece], 64, 1)
        after = pltpu.roll(window[8 + rows : 8 + rows + piece], 64, 1)
        right = jnp.where(lane < 64, swapped, after)
        left = jnp.where(lane < 64, before, swapped)
        shift[0] = window[7 : 7 + piece]
        shift[1] = window[9 : 9 + piece]
        shift[0, pl.ds(0, pairs, stride=rows), :] = halo_recv[k, 0, 0:pairs, :]
        shift[1, pl.ds(rows - 1, pairs, stride=rows), :] = halo_recv[k, 1, 0:pairs, :]
        flow = weights[0] * (mine - right) + weights[1] * (mine - left)
        flow = flow + weights[2] * (mine - shift[1]) + weights[3] * (mine - shift[0])
        return mine, flow * smooth

    for k in range(ITERS):
        mine, lap = laplace(k)
        drain(h_recv.at[k, pl.ds(0, h_count(k) - 1)], h_rsem.at[k])
        h_recv[k, seat] = h_send[k, seat]
        first = side * group if k == 0 else 0
        total = h_recv[k, first]
        for j in range(1, h_count(k)):
            total = total + h_recv[k, first + j]
        z_recv[k, zed] = total
        each(n_z - 1, lambda i: send_z(k, z_peer(i)).start())
        if k == ITERS - 1:
            for copy in c_copies:
                copy.start()
        drain(g_recv.at[k, pl.ds(0, g_count(k) - 1)], g_rsem.at[k])
        if k == 0:
            g_recv[k, mz] = g_send[k, strip]
        else:
            g_recv[k, y] = g_send[k, y]
        total = g_recv[k, 0]
        for j in range(1, g_count(k)):
            total = total + g_recv[k, j]
        vsq = jnp.sum(total[piece:, :])
        eta_u = 1.0 / (jnp.full((1, 128), vsq, F32) / rank + 8.0 * smooth + 1.0)
        mine = mine - eta_u * (total[0:piece, :] + lap)
        ubuf[k + 1, my_rows(), :] = mine
        if k + 1 < ITERS:
            each(n_y - 1, lambda i: send_u(k + 1, 2 * y_peer(i) + side).start())
            send_halos(k + 1, mine)
        else:
            each(n_mz - 1, lambda i: send_u(k + 1, mz_peer(i)).start())
        drain(z_recv.at[k, pl.ds(0, n_z - 1)], z_rsem.at[k])
        total = z_recv[k, 0]
        for j in range(1, n_z):
            total = total + z_recv[k, j]
        usq = jnp.sum(total[srows:, :])
        eta_v = 1.0 / (jnp.full((1, 128), usq, F32) / rank + 1.0)
        vbuf[k + 1, side, v_rows(), :] = vbuf[k, side, v_rows(), :] - eta_v * total[0:srows, :]
        peer = group_peer if k + 1 == ITERS else team_peer
        each(v_count(k + 1) - 1, lambda i: send_v(k + 1, peer(i)).start())
        if k == 0:
            thr_copy.wait()
            for copy in x_copies:
                copy.wait()
        if k + 1 == ITERS:
            for copy in c_copies:
                copy.wait()
        drain(ubuf.at[0, pl.ds(0, srows * (v_count(k + 1) - 1))], v_rsem.at[k])
        drain(ubuf.at[k + 1, pl.ds(8, piece * (u_count(k + 1) - 1))], u_rsem.at[k])
        if k + 1 < ITERS:
            usq = sweep(k + 1)
            start_g(k + 1)
            h_part(k + 1, usq)

    for t in range(cols // 2):
        u_in[:, 128 * t : 128 * (t + 1)] = ubuf[ITERS, 8 + rows * t : 8 + rows * (t + 1), :]
    v_in[...] = vbuf[ITERS, side]
    outs = [
        pltpu.make_async_copy(src, dst, out_sems.at[i])
        for i, (src, dst) in enumerate([(u_in, uo_ref), (v_in, vo_ref), (x_in, so_ref)])
    ]
    outs[0].start()
    outs[1].start()
    sweep(ITERS)
    for r in range(rows):
        for par in range(2):
            xf[pl.ds(r * cols + par, cols // 2, stride=2), :] = c_own[
                par, pl.ds(r, cols // 2, stride=rows), :
            ]
    x_in[...] = xf[...].astype(BF16).reshape(rows, cols, bins)
    outs[2].start()

    for k in range(ITERS):
        drain(g_send.at[k, pl.ds(0, g_count(k) - 1)], g_ssem.at[k])
        drain(h_send.at[k, pl.ds(0, h_count(k) - 1)], h_ssem.at[k])
        drain(z_recv.at[k, pl.ds(0, n_z - 1)], z_ssem.at[k])
        drain(ubuf.at[0, pl.ds(0, srows * (v_count(k + 1) - 1))], v_ssem.at[k])
        drain(ubuf.at[k + 1, pl.ds(8, piece * (u_count(k + 1) - 1))], u_ssem.at[k])
    for out in outs:
        out.wait()


def shards(group, spectra, scores, loadings, smooth, thresholds, across, down):
    rows, cols, bins = spectra.shape
    rank = loadings.shape[1]
    n_pix, n_mz = lax.axis_size("pix"), lax.axis_size("mz")
    nq = rows * cols // 2
    half = nq // 2
    piece = nq // n_mz
    edge = max(piece // rows, 8)
    srows = rank // group
    n_z, n_team = n_pix // group, 2 * group
    hbm = pl.BlockSpec(memory_space=pltpu.HBM)
    anywhere = pl.BlockSpec(memory_space=pl.ANY)
    dma = pltpu.SemaphoreType.DMA
    vmem = pltpu.VMEM
    args = (
        spectra, scores, loadings.T, smooth.reshape(1, rank), thresholds.reshape(1, bins),
        across, down,
    )
    out_shape = (
        jax.ShapeDtypeStruct(scores.shape, F32),
        jax.ShapeDtypeStruct((rank, bins), F32),
        jax.ShapeDtypeStruct(spectra.shape, BF16),
    )
    score_maps, final, sparse = pl.pallas_call(
        functools.partial(kernel, group),
        out_shape=out_shape,
        in_specs=[hbm] * 7,
        out_specs=(anywhere,) * 3,
        scratch_shapes=[
            vmem(spectra.shape, BF16),
            vmem(scores.shape, F32),
            vmem((rank, bins), F32),
            vmem((1, rank), F32),
            vmem((1, bins), F32),
            vmem(across.shape, jnp.int32),
            vmem(down.shape, jnp.int32),
            vmem(down.shape, jnp.int32),
            vmem((rows * cols, bins), F32),
            vmem((2, nq, bins), F32),
            vmem((2, half, bins), F32),
            vmem((2, nq, bins), F32),
            vmem((2, half, bins), F32),
            vmem((nq, 256), BF16),
            vmem((nq, 2 * bins), BF16),
            vmem((nq, 2 * bins), BF16),
            vmem((2, 256, 2 * bins), BF16),
            vmem((2, 256, 2 * bins), BF16),
            vmem((ITERS + 1, nq + 16, 128), F32),
            vmem((ITERS + 1, 2, rank, bins), F32),
            vmem((1, bins), F32),
            vmem((ITERS, n_mz, piece + 1, 128), F32),
            vmem((ITERS, n_mz, piece + 1, 128), F32),
            vmem((ITERS, n_team, srows + 8, 128), F32),
            vmem((ITERS, n_team, srows + 8, 128), F32),
            vmem((ITERS, n_z, srows + 8, 128), F32),
            vmem((ITERS, 4, edge, 128), F32),
            vmem((ITERS, 4, edge, 128), F32),
            vmem((piece, cols), F32),
            vmem((2, piece, 128), F32),
            vmem((4, piece, 128), F32),
            dma((7,)),
            dma((3,)),
        ]
        + [dma((ITERS,))] * 10
        + [dma((ITERS, 4))] * 2
        + [dma] * 4
        + [dma((2,))] * 4,
        compiler_params=pltpu.CompilerParams(
            collective_id=0, has_side_effects=True, vmem_limit_bytes=63 * 1024 * 1024
        ),
        cost_estimate=pl.CostEstimate(
            flops=2 * 10 * rows * cols * bins * rank * 3,
            bytes_accessed=2 * (spectra.size * 2 + scores.size * 4),
            transcendentals=0,
        ),
    )(*args)
    return score_maps, final.T, sparse


def solution(mesh, group=GROUP):
    in_specs = (
        P("pix", None, "mz"),
        P("pix", None),
        P("mz", None),
        P(),
        P("mz"),
        P("pix", None),
        P("pix", None),
    )
    out_specs = (P("pix", None), P("mz", None), P("pix", None, "mz"))
    return jax.shard_map(
        functools.partial(shards, group), mesh=mesh, in_specs=in_specs, out_specs=out_specs,
        check_vma=False,
    )
```

time: 79.6 us -> 68.7 us (0.86)
  Pallas kernels: 73.8 us -> 64.8 us
  local copies, waits for them, and re-layouts: 4.89 us -> 3.04 us
    pallas_call x1, Pallas kernels: 73.8 us -> 64.8 us  [shards(): pl.pallas_call(functools.partial(kernel, group), out_shape=out_shape, in_...]
    unnamed x15 -> x7, local copies, waits for them, and re-layouts: 4.19 us -> 3.04 us
where the time goes in v2:
time: 68.7 us; the launch traced here: 68.5 us
  Pallas kernels  64.8 us (94%)
  local copies, waits for them, and re-layouts  3.04 us (4%)
    pallas_call x1, Pallas kernels, shards(): pl.pallas_call(functools.partial(kernel, group), out_shape=out_shape, in_...  64.8 us
    unnamed x7, local copies, waits for them, and re-layouts  3.04 us

profile of v2, /device:TPU:1, one launch (start us, length us, event | category | flops | bytes accessed | tf_op | source)
XLA Modules:
  0.0 68.5 jit_solution(15936039659832550447)
XLA Ops:
  0.6 64.8 %shard_map.94 = (f32[4,16384]{1,0:T(4,128)}, f32[64,128]{1,0:T(8,128)}, bf16[4,256,128]{2,1,0:T(8,128)(2,1)}) custom-call(bf16[4,256,128]{2,1,0:T(8,128)(2,1)} %x_hbm.1, f32[4,16384]{1,0:T(4,128)} %u_hbm.1, f32[64,128]{1,0:T(8,128)} %bitcast.5, f32[1,64]{1,0:T(1,128)} %bitcast.6, f32[1,128]{1,0:T(1,128)} %bitcast.7, s32[4,256]{1,0:T(4,128)} %across_hbm.1, ...), custom_call_target="tpu_custom_call" | custom-call | flops 503316480 | bytes 1048576 | tf_op jit(solution)/shard_map/pallas_call | solution.py:475
  65.5 0.0 copy-start.1
  65.5 0.0 copy-start
  65.5 1.7 %copy.13 = f32[4,16384]{1,0:T(4,128)} copy(f32[4,16384]{1,0:T(4,128)} %get-tuple-element.12) | data formatting | bytes 524288
  67.2 0.0 copy-done.1
  67.2 0.6 copy.14
  67.8 0.0 copy-done
  67.8 0.7 %copy.15 = bf16[4,256,128]{2,1,0:T(8,128)(2,1)} copy(bf16[4,256,128]{2,1,0:T(8,128)(2,1)S(1)} %copy-done) | data formatting | bytes 524288
Async XLA Ops:
  65.5 1.7 %copy-start.1 = (f32[64,128]{1,0:T(8,128)S(1)}, f32[64,128]{1,0:T(8,128)}, u32[]{:S(2)}) copy-start(f32[64,128]{1,0:T(8,128)} %get-tuple-element.7) | copy-start | bytes 98308
  65.5 2.3 %copy-start = (bf16[4,256,128]{2,1,0:T(8,128)(2,1)S(1)}, bf16[4,256,128]{2,1,0:T(8,128)(2,1)}, u32[]{:S(2)}) copy-start(bf16[4,256,128]{2,1,0:T(8,128)(2,1)} %get-tuple-element.14) | copy-start | bytes 786436

commit v3 on v2

--- a/solution.py
+++ b/solution.py
@@ -34,7 +34,7 @@
     wtmp, shift, weights,
     in_sems, out_sems, g_ssem, g_rsem, u_ssem, u_rsem, h_ssem, h_rsem, z_ssem, z_rsem,
     v_ssem, v_rsem, halo_ssem, halo_rsem, down_ssem, down_rsem, thr_ssem, thr_rsem,
-    x_ssem, x_rsem, c_ssem, c_rsem,
+    x_ssem, x_rsem, c_ssem, c_rsem, cross_rsem,
 ):
     n_pix, n_mz = lax.axis_size("pix"), lax.axis_size("mz")
     pix, mz = lax.axis_index("pix"), lax.axis_index("mz")
@@ -165,18 +165,18 @@
             b_hl[slot, at : at + rank, 0:bins] = part
             b_hl[slot, at + rank : at + 2 * rank, bins : 2 * bins] = part
 
-    def sweep(k):
+    def sweep(k, which=None):
         paired = 0 < k < ITERS
         slots = (0, 1) if paired else (0,)
         vsq = jnp.zeros((1, 128), F32)
-        for slot in slots:
+        for slot in slots if which is None or which is side else ():
             factors(k, slot)
             v = vbuf[k, side if slot == 0 else 1 - side]
             vsq = vsq + jnp.sum(v * v, axis=0, keepdims=True)
         usq = zeros8
-        for q in range(0, half if paired else nq, chunk):
+        for q in range(0, nq if k == 0 else half, chunk):
             here = pl.ds(q, chunk)
-            own = half_rows(side, q, chunk) if paired else here
+            own = here if k == 0 else half_rows(side if which is None else which, q, chunk)
             u = ubuf[k, pl.ds(pl.multiple_of(own.start + 8, 8), chunk), :]
             u_h, u_l = split(u)
             u_hl[here, 0:128] = u_h
@@ -253,9 +253,10 @@
         ref = vbuf.at[k, side, v_rows()]
         return remote(ref, ref, v_ssem.at[k - 1], v_rsem.at[k - 1], team_device(j))
 
-    def send_u(k, to):
+    def send_u(k, to, rsem=None):
         ref = ubuf.at[k, my_rows()]
-        return remote(ref, ref, u_ssem.at[k - 1], u_rsem.at[k - 1], (pix, to))
+        rsem = u_rsem.at[k - 1] if rsem is None else rsem
+        return remote(ref, ref, u_ssem.at[k - 1], rsem, (pix, to))
 
     def g_count(k):
         return n_mz if k == 0 else n_y
@@ -287,8 +288,14 @@
         each(h_count(k) - 1, lambda i: send_h(k, peer(i)).start())
 
     usq = sweep(0)
-
     pl.semaphore_wait(barrier, n_mz - 1 + n_team - 1 + n_z - 1 + 2)
+    x_copies = [
+        remote(
+            x_own.at[par, half_rows(1 - side)], x_other.at[par], x_ssem.at[par], x_rsem.at[par],
+            twin,
+        )
+        for par in range(2)
+    ]
     start_g(0)
     h_part(0, usq)
     send_halos(0, ubuf[0, my_rows(), :])
@@ -297,15 +304,6 @@
     loads[4].wait()
     down_copy = remote(down_in, down_above, down_ssem, down_rsem, (below, mz))
     down_copy.start()
-    x_copies = [
-        remote(
-            x_own.at[par, half_rows(1 - side)], x_other.at[par], x_ssem.at[par], x_rsem.at[par],
-            twin,
-        )
-        for par in range(2)
-    ]
-    for copy in x_copies:
-        copy.start()
     c_copies = [
         remote(
             c_other.at[par], c_own.at[par, half_rows(side)], c_ssem.at[par], c_rsem.at[par],
@@ -378,9 +376,10 @@
             total = total + h_recv[k, first + j]
         z_recv[k, zed] = total
         each(n_z - 1, lambda i: send_z(k, z_peer(i)).start())
+        if k == 0:
+            x_copies[0].start()
         if k == ITERS - 1:
-            for copy in c_copies:
-                copy.start()
+            c_copies[1].start()
         drain(g_recv.at[k, pl.ds(0, g_count(k) - 1)], g_rsem.at[k])
         if k == 0:
             g_recv[k, mz] = g_send[k, strip]
@@ -396,8 +395,15 @@
         if k + 1 < ITERS:
             each(n_y - 1, lambda i: send_u(k + 1, 2 * y_peer(i) + side).start())
             send_halos(k + 1, mine)
+            if k == 0:
+                x_copies[1].start()
         else:
-            each(n_mz - 1, lambda i: send_u(k + 1, mz_peer(i)).start())
+            def both_sides(i):
+                send_u(k + 1, 2 * y_peer(i) + 1 - side, cross_rsem).start()
+                send_u(k + 1, 2 * y_peer(i) + side).start()
+
+            each(n_y - 1, both_sides)
+            send_u(k + 1, 2 * y + 1 - side, cross_rsem).start()
         drain(z_recv.at[k, pl.ds(0, n_z - 1)], z_rsem.at[k])
         total = z_recv[k, 0]
         for j in range(1, n_z):
@@ -411,26 +417,29 @@
             thr_copy.wait()
             for copy in x_copies:
                 copy.wait()
-        if k + 1 == ITERS:
-            for copy in c_copies:
-                copy.wait()
         drain(ubuf.at[0, pl.ds(0, srows * (v_count(k + 1) - 1))], v_rsem.at[k])
-        drain(ubuf.at[k + 1, pl.ds(8, piece * (u_count(k + 1) - 1))], u_rsem.at[k])
+        drain(ubuf.at[k + 1, pl.ds(8, piece * (n_y - 1))], u_rsem.at[k])
         if k + 1 < ITERS:
             usq = sweep(k + 1)
             start_g(k + 1)
             h_part(k + 1, usq)
-
-    for t in range(cols // 2):
-        u_in[:, 128 * t : 128 * (t + 1)] = ubuf[ITERS, 8 + rows * t : 8 + rows * (t + 1), :]
+            if k + 2 == ITERS:
+                c_copies[0].start()
+
+    sweep(ITERS, side)
     v_in[...] = vbuf[ITERS, side]
     outs = [
         pltpu.make_async_copy(src, dst, out_sems.at[i])
         for i, (src, dst) in enumerate([(u_in, uo_ref), (v_in, vo_ref), (x_in, so_ref)])
     ]
+    outs[1].start()
+    drain(ubuf.at[ITERS, pl.ds(8, piece * n_y)], cross_rsem)
+    for copy in c_copies:
+        copy.wait()
+    for t in range(cols // 2):
+        u_in[:, 128 * t : 128 * (t + 1)] = ubuf[ITERS, 8 + rows * t : 8 + rows * (t + 1), :]
     outs[0].start()
-    outs[1].start()
-    sweep(ITERS)
+    sweep(ITERS, 1 - side)
     for r in range(rows):
         for par in range(2):
             xf[pl.ds(r * cols + par, cols // 2, stride=2), :] = c_own[
@@ -446,6 +455,19 @@
         drain(ubuf.at[0, pl.ds(0, srows * (v_count(k + 1) - 1))], v_ssem.at[k])
         drain(ubuf.at[k + 1, pl.ds(8, piece * (u_count(k + 1) - 1))], u_ssem.at[k])
     for out in outs:
+        out.wait()
+
+
+def store(u_ref, v_ref, s_ref, uo_ref, vo_ref, so_ref, s, u, v, in_sems, out_sems):
+    order = [(s_ref, s, so_ref), (u_ref, u, uo_ref), (v_ref, v, vo_ref)]
+    loads = [pltpu.make_async_copy(a, b, in_sems.at[i]) for i, (a, b, _) in enumerate(order)]
+    stores = [pltpu.make_async_copy(b, c, out_sems.at[i]) for i, (_, b, c) in enumerate(order)]
+    for load in loads:
+        load.start()
+    for load, out in zip(loads, stores):
+        load.wait()
+        out.start()
+    for out in stores:
         out.wait()
 
 
@@ -472,7 +494,7 @@
         jax.ShapeDtypeStruct((rank, bins), F32),
         jax.ShapeDtypeStruct(spectra.shape, BF16),
     )
-    score_maps, final, sparse = pl.pallas_call(
+    outs = pl.pallas_call(
         functools.partial(kernel, group),
         out_shape=out_shape,
         in_specs=[hbm] * 7,
@@ -515,7 +537,8 @@
         + [dma((ITERS,))] * 10
         + [dma((ITERS, 4))] * 2
         + [dma] * 4
-        + [dma((2,))] * 4,
+        + [dma((2,))] * 4
+        + [dma],
         compiler_params=pltpu.CompilerParams(
             collective_id=0, has_side_effects=True, vmem_limit_bytes=63 * 1024 * 1024
         ),
@@ -525,6 +548,20 @@
             transcendentals=0,
         ),
     )(*args)
+    score_maps, final, sparse = pl.pallas_call(
+        store,
+        out_shape=out_shape,
+        in_specs=[hbm] * 3,
+        out_specs=(hbm,) * 3,
+        scratch_shapes=[
+            vmem(spectra.shape, BF16),
+            vmem(scores.shape, F32),
+            vmem((rank, bins), F32),
+            dma((3,)),
+            dma((3,)),
+        ],
+        compiler_params=pltpu.CompilerParams(vmem_limit_bytes=63 * 1024 * 1024),
+    )(*outs)
     return score_maps, final.T, sparse
 
 

time: 68.7 us -> 64 us (0.932)
  local copies, waits for them, and re-layouts: 3.04 us -> 0 us
  Pallas kernels: 64.8 us -> 63.3 us
    pallas_call x1, Pallas kernels: 64.8 us -> 61.5 us  [shards(): pl.pallas_call(functools.partial(kernel, group), out_shape=out_shape, in_...]
    unnamed x7 -> x0, local copies, waits for them, and re-layouts: 3.04 us -> none
    pallas_call x0 -> x1, Pallas kernels: none -> 1.79 us  [shards(): pl.pallas_call(store, out_shape=out_shape, in_specs=[hbm] * 3, out_specs=...]
where the time goes in v3:
time: 64 us; the launch traced here: 63.9 us
  Pallas kernels  63.3 us (99%)
  between operations  0.64 us (1%)
    pallas_call x1, Pallas kernels, shards(): pl.pallas_call(functools.partial(kernel, group), out_shape=out_shape, in_...  61.5 us
    pallas_call x1, Pallas kernels, shards(): pl.pallas_call(store, out_shape=out_shape, in_specs=[hbm] * 3, out_specs=...  1.79 us

profile of v3, /device:TPU:1, one launch (start us, length us, event | category | flops | bytes accessed | tf_op | source)
XLA Modules:
  0.0 63.9 jit_solution(16252664586822909900)
XLA Ops:
  0.6 61.5 %shard_map.94 = (f32[4,16384]{1,0:T(4,128)}, f32[64,128]{1,0:T(8,128)}, bf16[4,256,128]{2,1,0:T(8,128)(2,1)}) custom-call(bf16[4,256,128]{2,1,0:T(8,128)(2,1)} %x_hbm.1, f32[4,16384]{1,0:T(4,128)} %u_hbm.1, f32[64,128]{1,0:T(8,128)} %bitcast.4, f32[1,64]{1,0:T(1,128)} %bitcast.6, f32[1,128]{1,0:T(1,128)} %bitcast.7, s32[4,256]{1,0:T(4,128)} %across_hbm.1, ...), custom_call_target="tpu_custom_call" | custom-call | flops 503316480 | bytes 1048576 | tf_op jit(solution)/shard_map/pallas_call | solution.py:497
  62.1 1.8 %shard_map.95 = (f32[4,16384]{1,0:T(4,128)}, f32[64,128]{1,0:T(8,128)}, bf16[4,256,128]{2,1,0:T(8,128)(2,1)}) custom-call(f32[4,16384]{1,0:T(4,128)} %get-tuple-element.9.u_ref, f32[64,128]{1,0:T(8,128)} %get-tuple-element.10.v_ref, bf16[4,256,128]{2,1,0:T(8,128)(2,1)} %get-tuple-element.11.s_ref), custom_call_target="tpu_custom_call" | custom-call | tf_op jit(solution)/shard_map/pallas_call | solution.py:551

commit v4 on v3

--- a/solution.py
+++ b/solution.py
@@ -34,14 +34,14 @@
     wtmp, shift, weights,
     in_sems, out_sems, g_ssem, g_rsem, u_ssem, u_rsem, h_ssem, h_rsem, z_ssem, z_rsem,
     v_ssem, v_rsem, halo_ssem, halo_rsem, down_ssem, down_rsem, thr_ssem, thr_rsem,
-    x_ssem, x_rsem, c_ssem, c_rsem, cross_rsem,
+    x_ssem, x_rsem, c_ssem, c_rsem, cross_rsem, first_ssem, first_rsem,
 ):
     n_pix, n_mz = lax.axis_size("pix"), lax.axis_size("mz")
     pix, mz = lax.axis_index("pix"), lax.axis_index("mz")
-    n_z, n_y, n_team = n_pix // group, n_mz // 2, 2 * group
-    zed, spot = pix // group, pix % group
+    n_z, n_y = 2 * (n_pix // group), n_mz // 2
+    block, spot = pix // group, pix % group
     y, side = mz // 2, mz % 2
-    strip, seat = side * n_y + y, side * group + spot
+    strip, zed = side * n_y + y, 2 * block + side
     twin = (pix, 2 * y + 1 - side)
     rows, cols, bins = x_in.shape
     rank = v_in.shape[0]
@@ -69,17 +69,12 @@
     def mz_peer(i):
         return 2 * y_peer(i // 2) + (side + 1 - i % 2) % 2
 
-    def team_peer(i):
-        return (seat + i + 1) % n_team
-
-    def team_device(j):
-        return (zed * group + j % group, 2 * y + j // group)
-
-    def group_peer(i):
-        return side * group + (spot + i + 1) % group
-
-    def z_peer(i):
-        return (zed + i + 1) % n_z
+    def group_device(i):
+        return (block * group + far_first(spot, i, group), mz)
+
+    def z_device(i):
+        to = far_first(zed, i, n_z)
+        return (to // 2 * group + spot, 2 * y + to % 2)
 
     def strip_device(j):
         return (pix, 2 * (j % n_y) + j // n_y)
@@ -97,8 +92,8 @@
         load.start()
 
     each(n_mz - 1, lambda i: greet((pix, mz_peer(i))))
-    each(n_team - 1, lambda i: greet(team_device(team_peer(i))))
-    each(n_z - 1, lambda i: greet((z_peer(i) * group + spot, mz)))
+    each(group - 1, lambda i: greet(group_device(i)))
+    each(n_z - 1, lambda i: greet(z_device(i)))
     greet((below, mz))
     greet((above, mz))
 
@@ -235,23 +230,22 @@
             g_send.at[k, to], g_recv.at[k, y], g_ssem.at[k], g_rsem.at[k], (pix, 2 * to + side)
         )
 
-    def send_h(k, j):
+    def send_h(k, i):
         return remote(
-            h_send.at[k, j], h_recv.at[k, seat], h_ssem.at[k], h_rsem.at[k], team_device(j)
+            h_send.at[k, far_first(spot, i, group)], h_recv.at[k, spot], h_ssem.at[k],
+            h_rsem.at[k], group_device(i),
         )
 
-    def send_z(k, j):
-        return remote(
-            z_recv.at[k, zed], z_recv.at[k, zed], z_ssem.at[k], z_rsem.at[k],
-            (j * group + spot, mz),
-        )
+    def send_z(k, i):
+        ref = z_recv.at[k, zed]
+        return remote(ref, ref, z_ssem.at[k], z_rsem.at[k], z_device(i))
 
     def v_rows():
         return pl.ds(pl.multiple_of(srows * spot, 8), srows)
 
-    def send_v(k, j):
-        ref = vbuf.at[k, side, v_rows()]
-        return remote(ref, ref, v_ssem.at[k - 1], v_rsem.at[k - 1], team_device(j))
+    def send_v(k, i):
+        ref = vbuf.at[k, pl.ds(0, 2), v_rows()]
+        return remote(ref, ref, v_ssem.at[k - 1], v_rsem.at[k - 1], group_device(i))
 
     def send_u(k, to, rsem=None):
         ref = ubuf.at[k, my_rows()]
@@ -261,14 +255,8 @@
     def g_count(k):
         return n_mz if k == 0 else n_y
 
-    def h_count(k):
-        return group if k == 0 else n_team
-
     def u_count(k):
         return n_mz if k == ITERS else n_y
-
-    def v_count(k):
-        return group if k == ITERS else n_team
 
     def start_g(k):
         each(g_count(k) - 1, lambda i: send_g(k, i).start())
@@ -280,15 +268,23 @@
             both = mm(u_hl[0:n, :], d_h[dest, :], TN)
             prod = both[0:128, :] + both[128:256, :] + mm(u_hl[0:n, 0:128], d_l[dest, :], TN)
             h = prod[0:rank, 0:bins] + prod[rank : 2 * rank, bins : 2 * bins]
-            whose = side if slot == 0 else 1 - side
+            at = srows * (side if slot == 0 else 1 - side)
             for j in range(group):
-                h_send[k, whose * group + j, 0:srows, :] = h[j * srows : (j + 1) * srows, :]
-                h_send[k, whose * group + j, srows : srows + 8, :] = usq
-        peer = group_peer if k == 0 else team_peer
-        each(h_count(k) - 1, lambda i: send_h(k, peer(i)).start())
+                h_send[k, j, pl.ds(pl.multiple_of(at, 8), srows), :] = h[
+                    j * srows : (j + 1) * srows, :
+                ]
+        usq = jnp.sum(usq, axis=0, keepdims=True)
+        if k == 0:
+            usq = 0.5 * usq
+            at = pl.ds(pl.multiple_of(srows * (1 - side), 8), srows)
+            for j in range(group):
+                h_send[k, j, at, :] = jnp.zeros((srows, 128), F32)
+        for j in range(group):
+            h_send[k, j, 2 * srows : 2 * srows + 1, :] = usq
+        each(group - 1, lambda i: send_h(k, i).start())
 
     usq = sweep(0)
-    pl.semaphore_wait(barrier, n_mz - 1 + n_team - 1 + n_z - 1 + 2)
+    pl.semaphore_wait(barrier, n_mz - 1 + group - 1 + n_z - 1 + 2)
     x_copies = [
         remote(
             x_own.at[par, half_rows(1 - side)], x_other.at[par], x_ssem.at[par], x_rsem.at[par],
@@ -301,6 +297,9 @@
     send_halos(0, ubuf[0, my_rows(), :])
     thr_copy = remote(thr_in, thr_other, thr_ssem, thr_rsem, twin)
     thr_copy.start()
+    v_ref = vbuf.at[0, side]
+    v_copy = remote(v_ref, v_ref, first_ssem, first_rsem, twin)
+    v_copy.start()
     loads[4].wait()
     down_copy = remote(down_in, down_above, down_ssem, down_rsem, (below, mz))
     down_copy.start()
@@ -368,14 +367,13 @@
 
     for k in range(ITERS):
         mine, lap = laplace(k)
-        drain(h_recv.at[k, pl.ds(0, h_count(k) - 1)], h_rsem.at[k])
-        h_recv[k, seat] = h_send[k, seat]
-        first = side * group if k == 0 else 0
-        total = h_recv[k, first]
-        for j in range(1, h_count(k)):
-            total = total + h_recv[k, first + j]
+        drain(h_recv.at[k, pl.ds(0, group - 1)], h_rsem.at[k])
+        h_recv[k, spot] = h_send[k, spot]
+        total = h_recv[k, 0]
+        for j in range(1, group):
+            total = total + h_recv[k, j]
         z_recv[k, zed] = total
-        each(n_z - 1, lambda i: send_z(k, z_peer(i)).start())
+        each(n_z - 1, lambda i: send_z(k, i).start())
         if k == 0:
             x_copies[0].start()
         if k == ITERS - 1:
@@ -408,16 +406,20 @@
         total = z_recv[k, 0]
         for j in range(1, n_z):
             total = total + z_recv[k, j]
-        usq = jnp.sum(total[srows:, :])
+        usq = jnp.sum(total[2 * srows :, :])
         eta_v = 1.0 / (jnp.full((1, 128), usq, F32) / rank + 1.0)
-        vbuf[k + 1, side, v_rows(), :] = vbuf[k, side, v_rows(), :] - eta_v * total[0:srows, :]
-        peer = group_peer if k + 1 == ITERS else team_peer
-        each(v_count(k + 1) - 1, lambda i: send_v(k + 1, peer(i)).start())
+        if k == 0:
+            v_copy.wait()
+        for b in range(2):
+            vbuf[k + 1, b, v_rows(), :] = (
+                vbuf[k, b, v_rows(), :] - eta_v * total[b * srows : (b + 1) * srows, :]
+            )
+        each(group - 1, lambda i: send_v(k + 1, i).start())
         if k == 0:
             thr_copy.wait()
             for copy in x_copies:
                 copy.wait()
-        drain(ubuf.at[0, pl.ds(0, srows * (v_count(k + 1) - 1))], v_rsem.at[k])
+        drain(ubuf.at[0, pl.ds(0, 2 * srows * (group - 1))], v_rsem.at[k])
         drain(ubuf.at[k + 1, pl.ds(8, piece * (n_y - 1))], u_rsem.at[k])
         if k + 1 < ITERS:
             usq = sweep(k + 1)
@@ -450,9 +452,9 @@
 
     for k in range(ITERS):
         drain(g_send.at[k, pl.ds(0, g_count(k) - 1)], g_ssem.at[k])
-        drain(h_send.at[k, pl.ds(0, h_count(k) - 1)], h_ssem.at[k])
+        drain(h_send.at[k, pl.ds(0, group - 1)], h_ssem.at[k])
         drain(z_recv.at[k, pl.ds(0, n_z - 1)], z_ssem.at[k])
-        drain(ubuf.at[0, pl.ds(0, srows * (v_count(k + 1) - 1))], v_ssem.at[k])
+        drain(ubuf.at[0, pl.ds(0, 2 * srows * (group - 1))], v_ssem.at[k])
         drain(ubuf.at[k + 1, pl.ds(8, piece * (u_count(k + 1) - 1))], u_ssem.at[k])
     for out in outs:
         out.wait()
@@ -480,7 +482,7 @@
     piece = nq // n_mz
     edge = max(piece // rows, 8)
     srows = rank // group
-    n_z, n_team = n_pix // group, 2 * group
+    n_z = 2 * (n_pix // group)
     hbm = pl.BlockSpec(memory_space=pltpu.HBM)
     anywhere = pl.BlockSpec(memory_space=pl.ANY)
     dma = pltpu.SemaphoreType.DMA
@@ -523,9 +525,9 @@
             vmem((1, bins), F32),
             vmem((ITERS, n_mz, piece + 1, 128), F32),
             vmem((ITERS, n_mz, piece + 1, 128), F32),
-            vmem((ITERS, n_team, srows + 8, 128), F32),
-            vmem((ITERS, n_team, srows + 8, 128), F32),
-            vmem((ITERS, n_z, srows + 8, 128), F32),
+            vmem((ITERS, group, 2 * srows + 1, 128), F32),
+            vmem((ITERS, group, 2 * srows + 1, 128), F32),
+            vmem((ITERS, n_z, 2 * srows + 1, 128), F32),
             vmem((ITERS, 4, edge, 128), F32),
             vmem((ITERS, 4, edge, 128), F32),
             vmem((piece, cols), F32),
@@ -538,7 +540,7 @@
         + [dma((ITERS, 4))] * 2
         + [dma] * 4
         + [dma((2,))] * 4
-        + [dma],
+        + [dma] * 3,
         compiler_params=pltpu.CompilerParams(
             collective_id=0, has_side_effects=True, vmem_limit_bytes=63 * 1024 * 1024
         ),

time: 64 us -> 61.3 us (0.958)
  Pallas kernels: 63.3 us -> 60.5 us
    pallas_call x1, Pallas kernels: 61.5 us -> 58.7 us  [shards(): pl.pallas_call(functools.partial(kernel, group), out_shape=out_shape, in_...]
where the time goes in v4:
time: 61.3 us; the launch traced here: 61.2 us
  Pallas kernels  60.5 us (99%)
  between operations  0.64 us (1%)
    pallas_call x1, Pallas kernels, shards(): pl.pallas_call(functools.partial(kernel, group), out_shape=out_shape, in_...  58.7 us
    pallas_call x1, Pallas kernels, shards(): pl.pallas_call(store, out_shape=out_shape, in_specs=[hbm] * 3, out_specs=...  1.79 us

profile of v4, /device:TPU:1, one launch (start us, length us, event | category | flops | bytes accessed | tf_op | source)
XLA Modules:
  0.0 61.2 jit_solution(10094382348519694419)
XLA Ops:
  0.6 58.7 %shard_map.94 = (f32[4,16384]{1,0:T(4,128)}, f32[64,128]{1,0:T(8,128)}, bf16[4,256,128]{2,1,0:T(8,128)(2,1)}) custom-call(bf16[4,256,128]{2,1,0:T(8,128)(2,1)} %x_hbm.1, f32[4,16384]{1,0:T(4,128)} %u_hbm.1, f32[64,128]{1,0:T(8,128)} %bitcast.4, f32[1,64]{1,0:T(1,128)} %bitcast.6, f32[1,128]{1,0:T(1,128)} %bitcast.7, s32[4,256]{1,0:T(4,128)} %across_hbm.1, ...), custom_call_target="tpu_custom_call" | custom-call | flops 503316480 | bytes 1048576 | tf_op jit(solution)/shard_map/pallas_call | solution.py:499
  59.4 1.8 %shard_map.95 = (f32[4,16384]{1,0:T(4,128)}, f32[64,128]{1,0:T(8,128)}, bf16[4,256,128]{2,1,0:T(8,128)(2,1)}) custom-call(f32[4,16384]{1,0:T(4,128)} %get-tuple-element.9.u_ref, f32[64,128]{1,0:T(8,128)} %get-tuple-element.10.v_ref, bf16[4,256,128]{2,1,0:T(8,128)(2,1)} %get-tuple-element.11.s_ref), custom_call_target="tpu_custom_call" | custom-call | tf_op jit(solution)/shard_map/pallas_call | solution.py:553

commit v5 on v4

--- a/solution.py
+++ b/solution.py
@@ -197,7 +197,7 @@
                             t = t + old
                         clipped = jnp.clip(t, -thr, thr)
                         if k == ITERS:
-                            c[par, spot_rows, :] = t - clipped
+                            x_other[par, here, :] = t - clipped
                             continue
                         c[par, spot_rows, :] = clipped
                         d = -2.0 * clipped
@@ -423,18 +423,39 @@
         drain(ubuf.at[k + 1, pl.ds(8, piece * (n_y - 1))], u_rsem.at[k])
         if k + 1 < ITERS:
             usq = sweep(k + 1)
+            h_part(k + 1, usq)
             start_g(k + 1)
-            h_part(k + 1, usq)
             if k + 2 == ITERS:
                 c_copies[0].start()
+
+    def columns(which):
+        return pl.ds(pl.multiple_of(which * (cols // 2), 128), cols // 2)
+
+    def finish(which):
+        width = cols // 2
+        for r in range(rows):
+            for par in range(2):
+                xf[pl.ds(r * width + par, width // 2, stride=2), :] = x_other[
+                    par, pl.ds(r, width // 2, stride=rows), :
+                ]
+        for r in range(rows):
+            x_in[r, columns(which), :] = xf[r * width : (r + 1) * width, :].astype(BF16)
+        return out_half(which)
+
+    def out_half(which):
+        return pltpu.make_async_copy(
+            x_in.at[:, columns(which), :], so_ref.at[:, columns(which), :],
+            out_sems.at[2 + (which + side) % 2],
+        )
 
     sweep(ITERS, side)
     v_in[...] = vbuf[ITERS, side]
     outs = [
         pltpu.make_async_copy(src, dst, out_sems.at[i])
-        for i, (src, dst) in enumerate([(u_in, uo_ref), (v_in, vo_ref), (x_in, so_ref)])
+        for i, (src, dst) in enumerate([(u_in, uo_ref), (v_in, vo_ref)])
     ]
     outs[1].start()
+    finish(side).start()
     drain(ubuf.at[ITERS, pl.ds(8, piece * n_y)], cross_rsem)
     for copy in c_copies:
         copy.wait()
@@ -442,13 +463,7 @@
         u_in[:, 128 * t : 128 * (t + 1)] = ubuf[ITERS, 8 + rows * t : 8 + rows * (t + 1), :]
     outs[0].start()
     sweep(ITERS, 1 - side)
-    for r in range(rows):
-        for par in range(2):
-            xf[pl.ds(r * cols + par, cols // 2, stride=2), :] = c_own[
-                par, pl.ds(r, cols // 2, stride=rows), :
-            ]
-    x_in[...] = xf[...].astype(BF16).reshape(rows, cols, bins)
-    outs[2].start()
+    finish(1 - side).start()
 
     for k in range(ITERS):
         drain(g_send.at[k, pl.ds(0, g_count(k) - 1)], g_ssem.at[k])
@@ -456,7 +471,7 @@
         drain(z_recv.at[k, pl.ds(0, n_z - 1)], z_ssem.at[k])
         drain(ubuf.at[0, pl.ds(0, 2 * srows * (group - 1))], v_ssem.at[k])
         drain(ubuf.at[k + 1, pl.ds(8, piece * (u_count(k + 1) - 1))], u_ssem.at[k])
-    for out in outs:
+    for out in outs + [out_half(side), out_half(1 - side)]:
         out.wait()
 
 
@@ -534,7 +549,7 @@
             vmem((2, piece, 128), F32),
             vmem((4, piece, 128), F32),
             dma((7,)),
-            dma((3,)),
+            dma((4,)),
         ]
         + [dma((ITERS,))] * 10
         + [dma((ITERS, 4))] * 2

time: 61.3 us -> 60.6 us (0.989)
  Pallas kernels: 60.5 us -> 59.8 us
    pallas_call x1, Pallas kernels: 58.7 us -> 58 us  [shards(): pl.pallas_call(functools.partial(kernel, group), out_shape=out_shape, in_...]
where the time goes in v5:
time: 60.6 us; the launch traced here: 60.5 us
  Pallas kernels  59.8 us (99%)
  between operations  0.64 us (1%)
    pallas_call x1, Pallas kernels, shards(): pl.pallas_call(functools.partial(kernel, group), out_shape=out_shape, in_...  58 us
    pallas_call x1, Pallas kernels, shards(): pl.pallas_call(store, out_shape=out_shape, in_specs=[hbm] * 3, out_specs=...  1.79 us

profile of v5, /device:TPU:1, one launch (start us, length us, event | category | flops | bytes accessed | tf_op | source)
XLA Modules:
  0.0 60.5 jit_solution(13966126396282177598)
XLA Ops:
  0.6 58.0 %shard_map.94 = (f32[4,16384]{1,0:T(4,128)}, f32[64,128]{1,0:T(8,128)}, bf16[4,256,128]{2,1,0:T(8,128)(2,1)}) custom-call(bf16[4,256,128]{2,1,0:T(8,128)(2,1)} %x_hbm.1, f32[4,16384]{1,0:T(4,128)} %u_hbm.1, f32[64,128]{1,0:T(8,128)} %bitcast.4, f32[1,64]{1,0:T(1,128)} %bitcast.6, f32[1,128]{1,0:T(1,128)} %bitcast.7, s32[4,256]{1,0:T(4,128)} %across_hbm.1, ...), custom_call_target="tpu_custom_call" | custom-call | flops 503316480 | bytes 1048576 | tf_op jit(solution)/shard_map/pallas_call | solution.py:514
  58.7 1.8 %shard_map.95 = (f32[4,16384]{1,0:T(4,128)}, f32[64,128]{1,0:T(8,128)}, bf16[4,256,128]{2,1,0:T(8,128)(2,1)}) custom-call(f32[4,16384]{1,0:T(4,128)} %get-tuple-element.9.u_ref, f32[64,128]{1,0:T(8,128)} %get-tuple-element.10.v_ref, bf16[4,256,128]{2,1,0:T(8,128)(2,1)} %get-tuple-element.11.s_ref), custom_call_target="tpu_custom_call" | custom-call | tf_op jit(solution)/shard_map/pallas_call | solution.py:568

commit v6 on v5

--- a/solution.py
+++ b/solution.py
@@ -163,11 +163,8 @@
     def sweep(k, which=None):
         paired = 0 < k < ITERS
         slots = (0, 1) if paired else (0,)
-        vsq = jnp.zeros((1, 128), F32)
         for slot in slots if which is None or which is side else ():
             factors(k, slot)
-            v = vbuf[k, side if slot == 0 else 1 - side]
-            vsq = vsq + jnp.sum(v * v, axis=0, keepdims=True)
         usq = zeros8
         for q in range(0, nq if k == 0 else half, chunk):
             here = pl.ds(q, chunk)
@@ -177,7 +174,6 @@
             u_hl[here, 0:128] = u_h
             u_hl[here, 128:256] = u_l
             usq = usq + jnp.sum((u * u).reshape(chunk // 8, 8, 128), axis=0)
-            g = None
             for slot in slots:
                 approx = mm(u_hl[here, :], b_hh[slot]) + mm(u_h, b_hl[slot, 128:256, :])
                 thr = (thr_other if slot else thr_in)[...]
@@ -206,17 +202,24 @@
                     high, low = split(d)
                     d_h[dest, lanes] = high
                     d_l[dest, lanes] = low
-                if k == ITERS:
-                    continue
+        return usq
+
+    def products(k):
+        slots = (0,) if k == 0 else (0, 1)
+        vsq = jnp.zeros((1, 128), F32)
+        for slot in slots:
+            v = vbuf[k, side if slot == 0 else 1 - side]
+            vsq = vsq + jnp.sum(v * v, axis=0, keepdims=True)
+        for q in range(0, nq if k == 0 else half, chunk):
+            g = None
+            for slot in slots:
+                dest = pl.ds(slot * half + q, chunk)
                 g2 = mm(d_h[dest, :], b_hl[slot], NT)
                 part = g2[:, 0:128] + g2[:, 128:256] + mm(d_l[dest, :], b_hh[slot, 0:128, :], NT)
                 g = part if g is None else g + part
-            if k == ITERS:
-                continue
             for j in range(q // piece, (q + chunk) // piece):
                 g_send[k, j, 0:piece, :] = g[j * piece - q : (j + 1) * piece - q, :]
                 g_send[k, j, piece : piece + 1, :] = vsq
-        return usq
 
     def send_g(k, i):
         if k == 0:
@@ -284,6 +287,7 @@
         each(group - 1, lambda i: send_h(k, i).start())
 
     usq = sweep(0)
+    products(0)
     pl.semaphore_wait(barrier, n_mz - 1 + group - 1 + n_z - 1 + 2)
     x_copies = [
         remote(
@@ -424,6 +428,7 @@
         if k + 1 < ITERS:
             usq = sweep(k + 1)
             h_part(k + 1, usq)
+            products(k + 1)
             start_g(k + 1)
             if k + 2 == ITERS:
                 c_copies[0].start()

time: 60.6 us -> 61 us (level)
  no operation moved by 1% of the time
where the time goes in v6:
time: 61 us; the launch traced here: 60.9 us
  Pallas kernels  60.2 us (99%)
  between operations  0.64 us (1%)
    pallas_call x1, Pallas kernels, shards(): pl.pallas_call(functools.partial(kernel, group), out_shape=out_shape, in_...  58.4 us
    pallas_call x1, Pallas kernels, shards(): pl.pallas_call(store, out_shape=out_shape, in_specs=[hbm] * 3, out_specs=...  1.79 us

profile of v6, /device:TPU:1, one launch (start us, length us, event | category | flops | bytes accessed | tf_op | source)
XLA Modules:
  0.0 60.9 jit_solution(3903451659070301509)
XLA Ops:
  0.6 58.4 %shard_map.94 = (f32[4,16384]{1,0:T(4,128)}, f32[64,128]{1,0:T(8,128)}, bf16[4,256,128]{2,1,0:T(8,128)(2,1)}) custom-call(bf16[4,256,128]{2,1,0:T(8,128)(2,1)} %x_hbm.1, f32[4,16384]{1,0:T(4,128)} %u_hbm.1, f32[64,128]{1,0:T(8,128)} %bitcast.4, f32[1,64]{1,0:T(1,128)} %bitcast.6, f32[1,128]{1,0:T(1,128)} %bitcast.7, s32[4,256]{1,0:T(4,128)} %across_hbm.1, ...), custom_call_target="tpu_custom_call" | custom-call | flops 503316480 | bytes 1048576 | tf_op jit(solution)/shard_map/pallas_call | solution.py:519
  59.1 1.8 %shard_map.95 = (f32[4,16384]{1,0:T(4,128)}, f32[64,128]{1,0:T(8,128)}, bf16[4,256,128]{2,1,0:T(8,128)(2,1)}) custom-call(f32[4,16384]{1,0:T(4,128)} %get-tuple-element.9.u_ref, f32[64,128]{1,0:T(8,128)} %get-tuple-element.10.v_ref, bf16[4,256,128]{2,1,0:T(8,128)(2,1)} %get-tuple-element.11.s_ref), custom_call_target="tpu_custom_call" | custom-call | tf_op jit(solution)/shard_map/pallas_call | solution.py:573
